TPU v7x, 32 devices: a whole 2x2x4 slice. The times are simulated.
32 devices in a mesh: section: 8 (over z, y), dp: 4 (over x, core).
Axes of the slice: x: 2, y: 2, z: 4, core: 2. Of those that a mesh axis runs over, the one named last changes fastest.
Arguments:
- tokens: bfloat16 [1024, 960], P('dp'), may hold values from -16 to 16
- cotangent: bfloat16 [1024, 960], P('dp'), may hold values from -6 to 6
- seq_counts: int32 [16, 2], P('dp'), may hold values from 0 to 4, as said below
- attn_gain: float32 [8, 960], P('section'), may hold values from 0.25 to 1.75
- w_qkv: bfloat16 [8, 960, 1600], P('section'), may hold values from -0.1875 to 0.1875
- w_out: bfloat16 [8, 960, 960], P('section'), may hold values from -0.75 to 0.75
- ffn_gain: float32 [8, 960], P('section'), may hold values from 0.25 to 1.75
- w_gate_up: bfloat16 [8, 960, 5120], P('section'), may hold values from -0.1875 to 0.1875
- w_down: bfloat16 [8, 2560, 960], P('section'), may hold values from -0.125 to 0.125
Outputs:
- section_outputs: bfloat16 [8, 1024, 960], P('section', 'dp')
- section_input_grads: bfloat16 [8, 1024, 960], P('section', 'dp')
- attn_gain_grad: float32 [8, 960], P('section', 'dp')
- w_qkv_grad: float32 [8, 960, 1600], P('section', 'dp')
- w_out_grad: float32 [8, 960, 960], P('section', None, 'dp')
- ffn_gain_grad: float32 [8, 960], P('section', 'dp')
- w_gate_up_grad: float32 [8, 960, 5120], P('section', 'dp')
- w_down_grad: float32 [8, 2560, 960], P('section', None, 'dp')
Inputs may be any that keep to these rules, and one draw needn't show every extreme that they name: `seq_counts`: column 0 is the number of 64-token sequences (0 or 1) and column 1 the number of 16-token sequences of a micro-batch, laid from its first slot: a micro-batch holds one long sequence or two to four short ones. Every data group has a micro-batch with a long sequence and one with four short ones.
All inputs are finite; a program needn't handle non-finite values.
Results may differ from a plain program's by a relative error of at most 0.035.
Values may be sent and summed in bfloat16 or wider, within the bound.
A program may use at most 320 MiB of HBM per device.

v0:
```python
import jax
import jax.numpy as jnp
from jax import lax
from jax.sharding import PartitionSpec as P

HEADS = 15
KV_HEADS = 5
HEAD_DIM = 64
FF = 2560
SHORT_LEN = 16
LONG_LEN = 64


EPS = 1e-05
BASE = 10000.0
NEG = -1e30


def from_behind(value, axis, steps):
    count = lax.axis_size(axis)
    leading, last = (max(0, -steps), min(count, count - steps))
    return lax.ppermute(value, axis, [(source, source + steps) for source in range(leading, last)])


def layout(counts, length, short_len):
    slot_ids = jnp.arange(length, dtype=jnp.int32)
    piece_ids = slot_ids // short_len
    is_long = counts[0] > 0
    valid_mask = jnp.where(is_long, True, piece_ids < counts[1])
    document = jnp.where(is_long, 0, piece_ids)
    document = jnp.where(valid_mask, document, length + slot_ids)
    position = jnp.where(is_long, slot_ids, slot_ids % short_len)
    return (document, position, valid_mask)


def rotary(position, head_dim):
    half_dim = head_dim // 2
    frequency = BASE ** (-2.0 * jnp.arange(half_dim, dtype=jnp.float32) / head_dim)
    angles = position.astype(jnp.float32)[:, None] * frequency[None, :]
    return (jnp.cos(angles), jnp.sin(angles))


def rotate(heads_in, cosine, sine_part):
    half_dim = heads_in.shape[-1] // 2
    first = heads_in[..., :half_dim]
    second = heads_in[..., half_dim:]
    cos_wide = cosine[:, None, :]
    sin_wide = sine_part[:, None, :]
    return jnp.concatenate(
        [first * cos_wide - second * sin_wide, second * cos_wide + first * sin_wide], -1
    )


def rotate_back(grads_in, cosine, sine_part):
    half_dim = grads_in.shape[-1] // 2
    first = grads_in[..., :half_dim]
    second = grads_in[..., half_dim:]
    cos_wide = cosine[:, None, :]
    sin_wide = sine_part[:, None, :]
    return jnp.concatenate(
        [first * cos_wide + second * sin_wide, second * cos_wide - first * sin_wide], -1
    )


def make_table(counts):
    document, position, valid_mask = layout(counts, LONG_LEN, SHORT_LEN)
    slot_ids = jnp.arange(LONG_LEN, dtype=jnp.int32)
    allowed = (document[:, None] == document[None, :]) & (slot_ids[:, None] >= slot_ids[None, :])
    cosine, sine_part = rotary(position, HEAD_DIM)
    return (allowed, cosine, sine_part, valid_mask.astype(jnp.float32)[:, None])


def dot_t(left_side, right_side):
    return lax.dot_general(
        left_side, right_side, (((1,), (1,)), ((), ())), preferred_element_type=jnp.float32
    )


def dot_tn(left_side, right_side):
    return lax.dot_general(
        left_side, right_side, (((0,), (0,)), ((), ())), preferred_element_type=jnp.float32
    )


def rms_back(stream, inverse, gain, grad_normed):
    scaled = grad_normed * gain
    return inverse * scaled - stream * inverse**3 * jnp.mean(stream * scaled, -1, keepdims=True)


def block_forward(stream, weights, mask_table):
    gain_attn, w_qkv, w_out, gain_ffn, w_gate_up, w_down = weights
    allowed, cosine, sine_part, valid_col = mask_table
    num_rows = stream.shape[0]
    q_width = HEADS * HEAD_DIM
    kv_width = KV_HEADS * HEAD_DIM
    repeat = HEADS // KV_HEADS
    score_scale = HEAD_DIM ** (-0.5)
    inv_attn = lax.rsqrt(jnp.mean(stream * stream, -1, keepdims=True) + EPS)
    normed = (stream * inv_attn * gain_attn).astype(jnp.bfloat16)
    qkv_proj = jnp.dot(normed, w_qkv, preferred_element_type=jnp.float32)
    queries = rotate(qkv_proj[:, :q_width].reshape(num_rows, HEADS, HEAD_DIM), cosine, sine_part)
    queries = queries.astype(jnp.bfloat16).reshape(num_rows, KV_HEADS, repeat, HEAD_DIM)
    key_heads = rotate(
        qkv_proj[:, q_width : q_width + kv_width].reshape(num_rows, KV_HEADS, HEAD_DIM),
        cosine,
        sine_part,
    )
    key_heads = key_heads.astype(jnp.bfloat16)
    value_heads = (
        qkv_proj[:, q_width + kv_width :].reshape(num_rows, KV_HEADS, HEAD_DIM).astype(jnp.bfloat16)
    )
    scores = (
        jnp.einsum("qgrd,kgd->grqk", queries, key_heads, preferred_element_type=jnp.float32)
        * score_scale
    )
    scores = jnp.where(allowed, scores, NEG)
    row_max = jnp.max(scores, -1, keepdims=True)
    log_total = row_max + jnp.log(jnp.sum(jnp.exp(scores - row_max), -1, keepdims=True))
    probabilities = jnp.exp(scores - log_total)
    prob_low = probabilities.astype(jnp.bfloat16)
    mixed_heads = jnp.einsum(
        "grqk,kgd->qgrd", prob_low, value_heads, preferred_element_type=jnp.float32
    )
    mixed_heads = mixed_heads.reshape(num_rows, q_width).astype(jnp.bfloat16)
    middle = stream + jnp.dot(mixed_heads, w_out, preferred_element_type=jnp.float32)
    inv_ffn = lax.rsqrt(jnp.mean(middle * middle, -1, keepdims=True) + EPS)
    normed_ffn = (middle * inv_ffn * gain_ffn).astype(jnp.bfloat16)
    gate_up = jnp.dot(normed_ffn, w_gate_up, preferred_element_type=jnp.float32)
    gate_part = gate_up[:, :FF]
    up_part = gate_up[:, FF:]
    hidden = (gate_part * jax.nn.sigmoid(gate_part) * up_part).astype(jnp.bfloat16)
    output = middle + jnp.dot(hidden, w_down, preferred_element_type=jnp.float32)
    saved_parts = (
        stream,
        inv_attn,
        normed,
        queries,
        key_heads,
        value_heads,
        probabilities,
        prob_low,
        mixed_heads,
        middle,
        inv_ffn,
        normed_ffn,
        gate_part,
        up_part,
        hidden,
    )
    return (output, saved_parts)


def block_backward(saved_parts, grad_out, weights, mask_table):
    gain_attn, w_qkv, w_out, gain_ffn, w_gate_up, w_down = weights
    allowed, cosine, sine_part, valid_col = mask_table
    (
        stream,
        inv_attn,
        normed,
        queries,
        key_heads,
        value_heads,
        probabilities,
        prob_low,
        mixed_heads,
        middle,
        inv_ffn,
        normed_ffn,
        gate_part,
        up_part,
        hidden,
    ) = saved_parts
    num_rows = stream.shape[0]
    q_width = HEADS * HEAD_DIM
    kv_width = KV_HEADS * HEAD_DIM
    repeat = HEADS // KV_HEADS
    score_scale = HEAD_DIM ** (-0.5)
    grad_ffn = grad_out.astype(jnp.bfloat16)
    grad_hidden = dot_t(grad_ffn, w_down)
    sigmoid_gate = jax.nn.sigmoid(gate_part)
    grad_gate = grad_hidden * up_part * sigmoid_gate * (1.0 + gate_part * (1.0 - sigmoid_gate))
    grad_up = grad_hidden * gate_part * sigmoid_gate
    grad_gate_up = jnp.concatenate([grad_gate, grad_up], 1).astype(jnp.bfloat16)
    grad_normed_ffn = dot_t(grad_gate_up, w_gate_up)
    grad_middle = grad_out + rms_back(middle, inv_ffn, gain_ffn, grad_normed_ffn)
    gain_ffn_grad = jnp.sum(grad_normed_ffn * middle * inv_ffn, 0)
    grad_attn = grad_middle.astype(jnp.bfloat16)
    grad_mixed = (
        dot_t(grad_attn, w_out).astype(jnp.bfloat16).reshape(num_rows, KV_HEADS, repeat, HEAD_DIM)
    )
    grad_probs = jnp.einsum(
        "qgrd,kgd->grqk", grad_mixed, value_heads, preferred_element_type=jnp.float32
    )
    grad_values = jnp.einsum(
        "grqk,qgrd->kgd", prob_low, grad_mixed, preferred_element_type=jnp.float32
    )
    grad_scores = probabilities * (
        grad_probs - jnp.sum(grad_probs * probabilities, -1, keepdims=True)
    )
    grad_scores = grad_scores.astype(jnp.bfloat16)
    grad_queries = (
        jnp.einsum("grqk,kgd->qgrd", grad_scores, key_heads, preferred_element_type=jnp.float32)
        * score_scale
    )
    grad_keys = (
        jnp.einsum("grqk,qgrd->kgd", grad_scores, queries, preferred_element_type=jnp.float32)
        * score_scale
    )
    grad_queries = rotate_back(grad_queries.reshape(num_rows, HEADS, HEAD_DIM), cosine, sine_part)
    grad_keys = rotate_back(grad_keys, cosine, sine_part)
    grad_qkv = jnp.concatenate(
        [
            grad_queries.reshape(num_rows, q_width),
            grad_keys.reshape(num_rows, kv_width),
            grad_values.reshape(num_rows, kv_width),
        ],
        1,
    ).astype(jnp.bfloat16)
    grad_normed = dot_t(grad_qkv, w_qkv)
    grad_stream = grad_middle + rms_back(stream, inv_attn, gain_attn, grad_normed)
    gain_attn_grad = jnp.sum(grad_normed * stream * inv_attn, 0)
    return (
        grad_stream,
        (
            (normed, mixed_heads, normed_ffn, hidden),
            (grad_qkv, grad_attn, grad_gate_up, grad_ffn),
            gain_attn_grad,
            gain_ffn_grad,
        ),
    )


def pair_backward(block_in, block_mid, grad_out, weights, mask_table):
    saved_late = block_forward(block_mid, weights, mask_table)[1]
    grad_mid, late_parts = block_backward(saved_late, grad_out, weights, mask_table)
    saved_early = block_forward(block_in, weights, mask_table)[1]
    grad_in, early_parts = block_backward(saved_early, grad_mid, weights, mask_table)
    inputs_joined = tuple(
        (
            jnp.concatenate([early_item, late_item], 0)
            for early_item, late_item in zip(early_parts[0], late_parts[0])
        )
    )
    grads_joined = tuple(
        (
            jnp.concatenate([early_item, late_item], 0)
            for early_item, late_item in zip(early_parts[1], late_parts[1])
        )
    )
    return (
        grad_in,
        (
            inputs_joined,
            grads_joined,
            early_parts[2] + late_parts[2],
            early_parts[3] + late_parts[3],
        ),
    )


def store_at(buffer, update, slot_index, active):
    previous = lax.dynamic_index_in_dim(buffer, slot_index, 0, keepdims=False)
    return lax.dynamic_update_index_in_dim(
        buffer, jnp.where(active, update, previous), slot_index, 0
    )


def body(tokens, cotangent, seq_counts, attn_gain, w_qkv, w_out, ffn_gain, w_gate_up, w_down):
    weights = (attn_gain[0], w_qkv[0], w_out[0], ffn_gain[0], w_gate_up[0], w_down[0])
    sections = lax.axis_size("section")
    section_index = lax.axis_index("section")
    block_rows = LONG_LEN
    micros = tokens.shape[0] // block_rows
    width = tokens.shape[1]
    step_count = micros + sections - 1
    token_blocks = tokens.reshape(micros, block_rows, width)
    cot_blocks = cotangent.reshape(micros, block_rows, width)
    empty_sent = jnp.zeros((block_rows, width), jnp.bfloat16)
    empty_kept = jnp.zeros((micros, block_rows, width), jnp.float32)
    empty_out = jnp.zeros((micros, block_rows, width), jnp.bfloat16)

    def forward_step(loop_state, step_num):
        received, kept_in, kept_mid, outputs = loop_state
        micro_index = step_num - section_index
        active = (micro_index >= 0) & (micro_index < micros)
        slot_index = jnp.clip(micro_index, 0, micros - 1)
        fresh = lax.dynamic_index_in_dim(token_blocks, slot_index, 0, keepdims=False)
        block_in = jnp.where(section_index == 0, fresh, received).astype(jnp.float32)
        mask_table = make_table(lax.dynamic_index_in_dim(seq_counts, slot_index, 0, keepdims=False))

        def forward_compute(stream):
            block_mid = block_forward(stream, weights, mask_table)[0]
            final_out = block_forward(block_mid, weights, mask_table)[0] * mask_table[3]
            return (block_mid, final_out.astype(jnp.bfloat16))

        def forward_skipped(stream):
            return (jnp.zeros_like(stream), jnp.zeros((block_rows, width), jnp.bfloat16))

        block_mid, sent_out = lax.cond(active, forward_compute, forward_skipped, block_in)
        kept_in = store_at(kept_in, block_in, slot_index, active)
        kept_mid = store_at(kept_mid, block_mid, slot_index, active)
        outputs = store_at(outputs, sent_out, slot_index, active)
        received = from_behind(sent_out, "section", 1)
        return ((received, kept_in, kept_mid, outputs), None)

    forward_state, _ = lax.scan(
        forward_step,
        (empty_sent, empty_kept, empty_kept, empty_out),
        jnp.arange(step_count, dtype=jnp.int32),
    )
    kept_in = forward_state[1]
    kept_mid = forward_state[2]
    outputs = forward_state[3]
    weight_shapes = (w_qkv.shape[1:], w_out.shape[1:], w_gate_up.shape[1:], w_down.shape[1:])
    store_init = (
        tuple((jnp.zeros(shape_item, jnp.float32) for shape_item in weight_shapes)),
        jnp.zeros((width,), jnp.float32),
        jnp.zeros((width,), jnp.float32),
    )

    def absorb(store_now, parts):
        totals = tuple(
            (
                total_item + dot_tn(input_item, grad_item)
                for total_item, input_item, grad_item in zip(store_now[0], parts[0], parts[1])
            )
        )
        return (totals, store_now[1] + parts[2], store_now[2] + parts[3])

    def backward_step(loop_state, step_num):
        received, grads_in, store_now = loop_state
        offset = step_num - (sections - 1 - section_index)
        active = (offset >= 0) & (offset < micros)
        slot_index = jnp.clip(micros - 1 - offset, 0, micros - 1)
        from_loss = lax.dynamic_index_in_dim(cot_blocks, slot_index, 0, keepdims=False)
        incoming = jnp.where(section_index == sections - 1, from_loss, received).astype(jnp.float32)
        mask_table = make_table(lax.dynamic_index_in_dim(seq_counts, slot_index, 0, keepdims=False))
        block_in = lax.dynamic_index_in_dim(kept_in, slot_index, 0, keepdims=False)
        block_mid = lax.dynamic_index_in_dim(kept_mid, slot_index, 0, keepdims=False)

        def backward_compute(store_arg):
            grad_in, parts = pair_backward(
                block_in, block_mid, incoming * mask_table[3], weights, mask_table
            )
            return (grad_in.astype(jnp.bfloat16), absorb(store_arg, parts))

        def backward_skipped(store_arg):
            return (jnp.zeros((block_rows, width), jnp.bfloat16), store_arg)

        sent_back, store_now = lax.cond(active, backward_compute, backward_skipped, store_now)
        grads_in = store_at(grads_in, sent_back, slot_index, active)
        received = from_behind(sent_back, "section", -1)
        return ((received, grads_in, store_now), None)

    backward_state, _ = lax.scan(
        backward_step, (empty_sent, empty_out, store_init), jnp.arange(step_count, dtype=jnp.int32)
    )
    grads_in = backward_state[1]
    store_now = backward_state[2]
    grad_qkv, grad_out, grad_gate_up, grad_down, grad_gain_attn, grad_gain_ffn = store_now[0] + (
        store_now[1],
        store_now[2],
    )
    whole = (
        lax.psum(grad_qkv.astype(jnp.bfloat16), "dp").astype(jnp.float32),
        lax.psum(grad_out.astype(jnp.bfloat16), "dp").astype(jnp.float32),
        lax.psum(grad_gate_up.astype(jnp.bfloat16), "dp").astype(jnp.float32),
        lax.psum(grad_down.astype(jnp.bfloat16), "dp").astype(jnp.float32),
        lax.psum(grad_gain_attn.astype(jnp.bfloat16), "dp").astype(jnp.float32),
        lax.psum(grad_gain_ffn.astype(jnp.bfloat16), "dp").astype(jnp.float32),
    )
    share_rows = width // lax.axis_size("dp")
    begin_row = lax.axis_index("dp") * share_rows
    summed = (
        lax.dynamic_slice_in_dim(whole[0], begin_row, share_rows, 0),
        lax.dynamic_slice_in_dim(whole[1], begin_row, share_rows, 1),
        lax.dynamic_slice_in_dim(whole[2], begin_row, share_rows, 0),
        lax.dynamic_slice_in_dim(whole[3], begin_row, share_rows, 1),
        lax.dynamic_slice_in_dim(whole[4], begin_row, share_rows, 0),
        lax.dynamic_slice_in_dim(whole[5], begin_row, share_rows, 0),
    )
    section_outputs = outputs.reshape(1, micros * block_rows, width)
    section_input_grads = grads_in.reshape(1, micros * block_rows, width)
    return (
        section_outputs,
        section_input_grads,
        summed[4][None],
        summed[0][None],
        summed[1][None],
        summed[5][None],
        summed[2][None],
        summed[3][None],
    )


def solution(mesh):
    in_specs = (
        P("dp", None),
        P("dp", None),
        P("dp", None),
        P("section", None),
        P("section", None, None),
        P("section", None, None),
        P("section", None),
        P("section", None, None),
        P("section", None, None),
    )
    out_specs = (
        P("section", "dp", None),
        P("section", "dp", None),
        P("section", "dp"),
        P("section", "dp", None),
        P("section", None, "dp"),
        P("section", "dp"),
        P("section", "dp", None),
        P("section", None, "dp"),
    )
    return jax.shard_map(body, mesh=mesh, in_specs=in_specs, out_specs=out_specs, check_vma=False)
```

profile of v0, /device:TPU:0, one launch (start us, length us, event | category | flops | bytes accessed | tf_op | source)
XLA Modules:
  0.0 3332.2 jit_solution(10727985497502325482)
XLA Ops:
  11.3 8.0 copy.123
  23.5 636.2 %while.44 = (s32[]{:T(128)}, bf16[64,960]{1,0:T(8,128)(2,1)}, f32[4,64,960]{2,1,0:T(8,128)}, f32[4,64,960]{2,1,0:T(8,128)}, bf16[4,64,960]{2,1,0:T(8,128)(2,1)},...) while((s32[]{:T(128)}, bf16[64,960]{1,0:T(8,128)(2,1)}, ...), condition=%wide.region_11.12_spmd, body=%wide.region_0.11_spmd.sunk | while | flops 2554220288 | bytes 110342328 | solution.py:306
  30.8 58.5 %conditional.4 = (f32[64,960]{1,0:T(8,128)}, bf16[64,960]{1,0:T(8,128)(2,1)}) conditional(s32[]{:T(128)} %convert_element_type.432, () %tuple.238, (f32[64,960]{1,0:T(8,128)S(1)}, f32[1,960]{1,0:T(1,128)S(1)}, bf16[960,1600]{1,0:T(8,128)(2,1)S(1)}, pred[64,1]{0,1:T(4,128)(4,1)S(1)}, s32[64,1]{0,1:T(1,128)S(1)}, /*index=5*/s32[64,1]{0,1:T(1,128)S(1)}, ...), branch_computations={%region_1.1_spmd, %region_2.10_spmd} | conditional | flops 2553911296 | bytes 105923928 | solution.py:299
  53.7 6.0 fusion.21
  103.7 58.5 %conditional.4 = (f32[64,960]{1,0:T(8,128)}, bf16[64,960]{1,0:T(8,128)(2,1)}) conditional(s32[]{:T(128)} %convert_element_type.432, () %tuple.238, (f32[64,960]{1,0:T(8,128)S(1)}, f32[1,960]{1,0:T(1,128)S(1)}, bf16[960,1600]{1,0:T(8,128)(2,1)S(1)}, pred[64,1]{0,1:T(4,128)(4,1)S(1)}, s32[64,1]{0,1:T(1,128)S(1)}, /*index=5*/s32[64,1]{0,1:T(1,128)S(1)}, ...), branch_computations={%region_1.1_spmd, %region_2.10_spmd} | conditional | flops 2553911296 | bytes 105923928 | solution.py:299
  178.4 58.5 %conditional.4 = (f32[64,960]{1,0:T(8,128)}, bf16[64,960]{1,0:T(8,128)(2,1)}) conditional(s32[]{:T(128)} %convert_element_type.432, () %tuple.238, (f32[64,960]{1,0:T(8,128)S(1)}, f32[1,960]{1,0:T(1,128)S(1)}, bf16[960,1600]{1,0:T(8,128)(2,1)S(1)}, pred[64,1]{0,1:T(4,128)(4,1)S(1)}, s32[64,1]{0,1:T(1,128)S(1)}, /*index=5*/s32[64,1]{0,1:T(1,128)S(1)}, ...), branch_computations={%region_1.1_spmd, %region_2.10_spmd} | conditional | flops 2553911296 | bytes 105923928 | solution.py:299
  252.2 58.5 %conditional.4 = (f32[64,960]{1,0:T(8,128)}, bf16[64,960]{1,0:T(8,128)(2,1)}) conditional(s32[]{:T(128)} %convert_element_type.432, () %tuple.238, (f32[64,960]{1,0:T(8,128)S(1)}, f32[1,960]{1,0:T(1,128)S(1)}, bf16[960,1600]{1,0:T(8,128)(2,1)S(1)}, pred[64,1]{0,1:T(4,128)(4,1)S(1)}, s32[64,1]{0,1:T(1,128)S(1)}, /*index=5*/s32[64,1]{0,1:T(1,128)S(1)}, ...), branch_computations={%region_1.1_spmd, %region_2.10_spmd} | conditional | flops 2553911296 | bytes 105923928 | solution.py:299
  328.4 59.9 %collective-permute-start = (bf16[64,960]{1,0:T(8,128)(2,1)}, bf16[64,960]{1,0:T(8,128)(2,1)S(1)}, u32[]{:S(2)}, u32[]{:S(2)}) collective-permute-start(bf16[64,960]{1,0:T(8,128)(2,1)} %get-tuple-element.1528), channel_id=1, source_target_pairs={{0,4},{4,8},{8,12},{12,16},{16,20},{20,24},{24,28},{1,5},{5,9},{9,... | collective-permute-start | bytes 368648 | tf_op jit(solution)/shard_map/while/body/eval_jaxpr/ppermute | solution.py:22
  418.3 59.9 %collective-permute-start = (bf16[64,960]{1,0:T(8,128)(2,1)}, bf16[64,960]{1,0:T(8,128)(2,1)S(1)}, u32[]{:S(2)}, u32[]{:S(2)}) collective-permute-start(bf16[64,960]{1,0:T(8,128)(2,1)} %get-tuple-element.1528), channel_id=1, source_target_pairs={{0,4},{4,8},{8,12},{12,16},{16,20},{20,24},{24,28},{1,5},{5,9},{9,... | collective-permute-start | bytes 368648 | tf_op jit(solution)/shard_map/while/body/eval_jaxpr/ppermute | solution.py:22
  508.2 58.2 %collective-permute-start = (bf16[64,960]{1,0:T(8,128)(2,1)}, bf16[64,960]{1,0:T(8,128)(2,1)S(1)}, u32[]{:S(2)}, u32[]{:S(2)}) collective-permute-start(bf16[64,960]{1,0:T(8,128)(2,1)} %get-tuple-element.1528), channel_id=1, source_target_pairs={{0,4},{4,8},{8,12},{12,16},{16,20},{20,24},{24,28},{1,5},{5,9},{9,... | collective-permute-start | bytes 368648 | tf_op jit(solution)/shard_map/while/body/eval_jaxpr/ppermute | solution.py:22
  596.4 59.1 %collective-permute-start = (bf16[64,960]{1,0:T(8,128)(2,1)}, bf16[64,960]{1,0:T(8,128)(2,1)S(1)}, u32[]{:S(2)}, u32[]{:S(2)}) collective-permute-start(bf16[64,960]{1,0:T(8,128)(2,1)} %get-tuple-element.1528), channel_id=1, source_target_pairs={{0,4},{4,8},{8,12},{12,16},{16,20},{20,24},{24,28},{1,5},{5,9},{9,... | collective-permute-start | bytes 368648 | tf_op jit(solution)/shard_map/while/body/eval_jaxpr/ppermute | solution.py:22
  672.3 9.0 broadcast_in_dim.166
  681.4 2269.2 %while.45 = (s32[]{:T(128)}, bf16[64,960]{1,0:T(8,128)(2,1)}, bf16[4,64,960]{2,1,0:T(8,128)(2,1)}, f32[960,1600]{1,0:T(8,128)}, f32[960,960]{1,0:T(8,128)}, /*in...) while((s32[]{:T(128)}, bf16[64,960]{1,0:T(8,128)(2,1)}, ...), condition=%wide.region_33.34_spmd, body=%wide.region_12.33_spmd.sunk | while | flops 7053121536 | bytes 361742528 | solution.py:355
  725.4 58.4 %collective-permute-done.1 = bf16[64,960]{1,0:T(8,128)(2,1)S(1)} collective-permute-done((bf16[64,960]{1,0:T(8,128)(2,1)}, bf16[64,960]{1,0:T(8,128)(2,1)S(1)}, u32[]{:S(2)}, u32[]{:S(2)}) %collective-permute-start.1) | collective-permute-done | bytes 122912 | tf_op jit(solution)/shard_map/while/body/eval_jaxpr/ppermute | solution.py:22
  808.6 59.1 %collective-permute-done.1 = bf16[64,960]{1,0:T(8,128)(2,1)S(1)} collective-permute-done((bf16[64,960]{1,0:T(8,128)(2,1)}, bf16[64,960]{1,0:T(8,128)(2,1)S(1)}, u32[]{:S(2)}, u32[]{:S(2)}) %collective-permute-start.1) | collective-permute-done | bytes 122912 | tf_op jit(solution)/shard_map/while/body/eval_jaxpr/ppermute | solution.py:22
  892.6 58.2 %collective-permute-done.1 = bf16[64,960]{1,0:T(8,128)(2,1)S(1)} collective-permute-done((bf16[64,960]{1,0:T(8,128)(2,1)}, bf16[64,960]{1,0:T(8,128)(2,1)S(1)}, u32[]{:S(2)}, u32[]{:S(2)}) %collective-permute-start.1) | collective-permute-done | bytes 122912 | tf_op jit(solution)/shard_map/while/body/eval_jaxpr/ppermute | solution.py:22
  960.6 1229.5 %collective-permute-done.1 = bf16[64,960]{1,0:T(8,128)(2,1)S(1)} collective-permute-done((bf16[64,960]{1,0:T(8,128)(2,1)}, bf16[64,960]{1,0:T(8,128)(2,1)S(1)}, u32[]{:S(2)}, u32[]{:S(2)}) %collective-permute-start.1) | collective-permute-done | bytes 122912 | tf_op jit(solution)/shard_map/while/body/eval_jaxpr/ppermute | solution.py:22
  2196.5 175.8 %conditional.5 = (bf16[64,960]{1,0:T(8,128)(2,1)}, f32[960,1600]{1,0:T(8,128)}, f32[960,960]{1,0:T(8,128)}, f32[960,5120]{1,0:T(8,128)}, f32[2560,960]{0,1:T(8,128)}, /*index=5*/f32[960]{0:T(1024)S(1)}, f32[960]{0:T(1024)S(1)}) conditional(s32[]{:T(128)} %convert_element_type.436, (f32[960,1600]{1,0:T(8,128)}, f32[960,960]{1,0:T(8,128)}, ...), branch_computations={%region_13.13_spmd, %region_14.32_spmd} | conditional | flops 7052935680 | bytes 359601376 | solution.py:350
  2343.0 6.7 convolution_add_fusion.6
  2352.3 20.0 convolution_add_fusion.4
  2386.6 175.8 %conditional.5 = (bf16[64,960]{1,0:T(8,128)(2,1)}, f32[960,1600]{1,0:T(8,128)}, f32[960,960]{1,0:T(8,128)}, f32[960,5120]{1,0:T(8,128)}, f32[2560,960]{0,1:T(8,128)}, /*index=5*/f32[960]{0:T(1024)S(1)}, f32[960]{0:T(1024)S(1)}) conditional(s32[]{:T(128)} %convert_element_type.436, (f32[960,1600]{1,0:T(8,128)}, f32[960,960]{1,0:T(8,128)}, ...), branch_computations={%region_13.13_spmd, %region_14.32_spmd} | conditional | flops 7052935680 | bytes 359601376 | solution.py:350
  2533.2 6.7 convolution_add_fusion.6
  2542.4 20.0 convolution_add_fusion.4
  2576.7 175.8 %conditional.5 = (bf16[64,960]{1,0:T(8,128)(2,1)}, f32[960,1600]{1,0:T(8,128)}, f32[960,960]{1,0:T(8,128)}, f32[960,5120]{1,0:T(8,128)}, f32[2560,960]{0,1:T(8,128)}, /*index=5*/f32[960]{0:T(1024)S(1)}, f32[960]{0:T(1024)S(1)}) conditional(s32[]{:T(128)} %convert_element_type.436, (f32[960,1600]{1,0:T(8,128)}, f32[960,960]{1,0:T(8,128)}, ...), branch_computations={%region_13.13_spmd, %region_14.32_spmd} | conditional | flops 7052935680 | bytes 359601376 | solution.py:350
  2723.3 6.7 convolution_add_fusion.6
  2732.6 20.0 convolution_add_fusion.4
  2766.9 175.8 %conditional.5 = (bf16[64,960]{1,0:T(8,128)(2,1)}, f32[960,1600]{1,0:T(8,128)}, f32[960,960]{1,0:T(8,128)}, f32[960,5120]{1,0:T(8,128)}, f32[2560,960]{0,1:T(8,128)}, /*index=5*/f32[960]{0:T(1024)S(1)}, f32[960]{0:T(1024)S(1)}) conditional(s32[]{:T(128)} %convert_element_type.436, (f32[960,1600]{1,0:T(8,128)}, f32[960,960]{1,0:T(8,128)}, ...), branch_computations={%region_13.13_spmd, %region_14.32_spmd} | conditional | flops 7052935680 | bytes 359601376 | solution.py:350
  2913.4 6.7 convolution_add_fusion.6
  2922.7 20.0 convolution_add_fusion.4
  2962.9 11.7 convert_element_type.364
  2976.6 6.1 all-reduce
  2985.0 327.8 %all-reduce.4.cloned.1.call-done = (bf16[960,1600]{1,0:T(8,128)(2,1)}, bf16[960,960]{1,0:T(8,128)(2,1)}, bf16[960,5120]{1,0:T(8,128)(2,1)}, bf16[2560,960]{0,1:T(8,128)(2,1)}) async-done(((bf16[960,1600]{1,0:T(8,128)(2,1)}, bf16[960,960]{1,0:T(8,128)(2,1)}, bf16[960,5120]{1,0:T(8,128)(2,1)}, bf16[2560,960]{0,1:T(8,128)(2,1)}), (bf16[960,1600]{1,0:T(8,128)(2,1)}, bf16[960,960]{1,0:T(8,128)(2,1)}, ...) | async-done | bytes 19660816 | tf_op jit(solution)/shard_map/psum | solution.py:365
  (1857 shorter events, 1157.9 us)
Async XLA Ops:
  7.2 3305.6 %all-reduce.4.cloned.1.call-start = ((), (), s32[]{:S(2)}) async-start(), calls=%async_computation | async-start | bytes 39813120 | tf_op jit(solution)/shard_map/psum | solution.py:365
  89.3 6.5 collective-permute-start
  162.2 8.3 collective-permute-start
  236.9 7.4 collective-permute-start
  310.8 8.4 collective-permute-start
  328.4 63.3 %collective-permute-start = (bf16[64,960]{1,0:T(8,128)(2,1)}, bf16[64,960]{1,0:T(8,128)(2,1)S(1)}, u32[]{:S(2)}, u32[]{:S(2)}) collective-permute-start(bf16[64,960]{1,0:T(8,128)(2,1)} %get-tuple-element.1528), channel_id=1, source_target_pairs={{0,4},{4,8},{8,12},{12,16},{16,20},{20,24},{24,28},{1,5},{5,9},{9,... | collective-permute-start | bytes 368648 | tf_op jit(solution)/shard_map/while/body/eval_jaxpr/ppermute | solution.py:22
  401.0 8.0 collective-permute-start
  418.3 63.3 %collective-permute-start = (bf16[64,960]{1,0:T(8,128)(2,1)}, bf16[64,960]{1,0:T(8,128)(2,1)S(1)}, u32[]{:S(2)}, u32[]{:S(2)}) collective-permute-start(bf16[64,960]{1,0:T(8,128)(2,1)} %get-tuple-element.1528), channel_id=1, source_target_pairs={{0,4},{4,8},{8,12},{12,16},{16,20},{20,24},{24,28},{1,5},{5,9},{9,... | collective-permute-start | bytes 368648 | tf_op jit(solution)/shard_map/while/body/eval_jaxpr/ppermute | solution.py:22
  490.9 8.0 collective-permute-start
  508.2 61.5 %collective-permute-start = (bf16[64,960]{1,0:T(8,128)(2,1)}, bf16[64,960]{1,0:T(8,128)(2,1)S(1)}, u32[]{:S(2)}, u32[]{:S(2)}) collective-permute-start(bf16[64,960]{1,0:T(8,128)(2,1)} %get-tuple-element.1528), channel_id=1, source_target_pairs={{0,4},{4,8},{8,12},{12,16},{16,20},{20,24},{24,28},{1,5},{5,9},{9,... | collective-permute-start | bytes 368648 | tf_op jit(solution)/shard_map/while/body/eval_jaxpr/ppermute | solution.py:22
  579.1 8.0 collective-permute-start
  596.4 62.5 %collective-permute-start = (bf16[64,960]{1,0:T(8,128)(2,1)}, bf16[64,960]{1,0:T(8,128)(2,1)S(1)}, u32[]{:S(2)}, u32[]{:S(2)}) collective-permute-start(bf16[64,960]{1,0:T(8,128)(2,1)} %get-tuple-element.1528), channel_id=1, source_target_pairs={{0,4},{4,8},{8,12},{12,16},{16,20},{20,24},{24,28},{1,5},{5,9},{9,... | collective-permute-start | bytes 368648 | tf_op jit(solution)/shard_map/while/body/eval_jaxpr/ppermute | solution.py:22
  707.7 7.7 collective-permute-start.1
  722.5 61.3 %collective-permute-start.1 = (bf16[64,960]{1,0:T(8,128)(2,1)}, bf16[64,960]{1,0:T(8,128)(2,1)S(1)}, u32[]{:S(2)}, u32[]{:S(2)}) collective-permute-start(bf16[64,960]{1,0:T(8,128)(2,1)} %get-tuple-element.1557), channel_id=1, source_target_pairs={{4,0},{8,4},{12,8},{16,12},{20,16},{24,20},{28,24},{5,1},{9,5},{13... | collective-permute-start | bytes 368648 | tf_op jit(solution)/shard_map/while/body/eval_jaxpr/ppermute | solution.py:22
  790.8 8.0 collective-permute-start.1
  805.7 62.0 %collective-permute-start.1 = (bf16[64,960]{1,0:T(8,128)(2,1)}, bf16[64,960]{1,0:T(8,128)(2,1)S(1)}, u32[]{:S(2)}, u32[]{:S(2)}) collective-permute-start(bf16[64,960]{1,0:T(8,128)(2,1)} %get-tuple-element.1557), channel_id=1, source_target_pairs={{4,0},{8,4},{12,8},{16,12},{20,16},{24,20},{28,24},{5,1},{9,5},{13... | collective-permute-start | bytes 368648 | tf_op jit(solution)/shard_map/while/body/eval_jaxpr/ppermute | solution.py:22
  874.7 8.0 collective-permute-start.1
  889.7 61.1 %collective-permute-start.1 = (bf16[64,960]{1,0:T(8,128)(2,1)}, bf16[64,960]{1,0:T(8,128)(2,1)S(1)}, u32[]{:S(2)}, u32[]{:S(2)}) collective-permute-start(bf16[64,960]{1,0:T(8,128)(2,1)} %get-tuple-element.1557), channel_id=1, source_target_pairs={{4,0},{8,4},{12,8},{16,12},{20,16},{24,20},{28,24},{5,1},{9,5},{13... | collective-permute-start | bytes 368648 | tf_op jit(solution)/shard_map/while/body/eval_jaxpr/ppermute | solution.py:22
  957.7 1232.4 %collective-permute-start.1 = (bf16[64,960]{1,0:T(8,128)(2,1)}, bf16[64,960]{1,0:T(8,128)(2,1)S(1)}, u32[]{:S(2)}, u32[]{:S(2)}) collective-permute-start(bf16[64,960]{1,0:T(8,128)(2,1)} %get-tuple-element.1557), channel_id=1, source_target_pairs={{4,0},{8,4},{12,8},{16,12},{20,16},{24,20},{28,24},{5,1},{9,5},{13... | collective-permute-start | bytes 368648 | tf_op jit(solution)/shard_map/while/body/eval_jaxpr/ppermute | solution.py:22
  2352.3 20.0 copy-start.5
  2352.3 20.0 copy-start.62
  2352.3 20.0 copy-start.66
  2372.3 8.0 collective-permute-start.1
  2542.4 20.0 copy-start.5
  2542.4 20.0 copy-start.62
  2562.4 8.0 collective-permute-start.1
  2732.5 20.0 copy-start.5
  2732.6 20.0 copy-start.62
  2752.6 8.0 collective-permute-start.1
  2922.7 20.0 copy-start.5
  2922.7 20.0 copy-start.62
  2942.7 7.1 collective-permute-start.1
  (347 other events, 1851.9 us)
Sparse Core Ops, SparseCore 0:
  2974.7 337.9 all-reduce.3
where the time goes:
time: 3350 us; the launch traced here: 3330 us
  waiting for transfers between devices  1760 us (53%)
  local copies, waits for them, and re-layouts  525 us (16%)
  matrix products  450 us (13%)
  starting transfers between devices  275 us (8%)
  other arithmetic  241 us (7%)
  loops' own time  56.8 us (2%)
    ppermute x22, waiting for transfers between devices, from_behind(): lax.ppermute(value, axis, [(source, source + steps) for source in range(l...  1440 us
    psum x1, waiting for transfers between devices, body(): lax.psum(grad_qkv.astype(jnp.bfloat16), 'dp').astype(jnp.float32)  328 us
    ppermute x22, starting transfers between devices, from_behind(): lax.ppermute(value, axis, [(source, source + steps) for source in range(l...  275 us
    dot_general x16, matrix products, dot_tn(): lax.dot_general(left_side, right_side, (((0,), (0,)), ((), ())), preferre...  137 us
    cond x704, local copies, waits for them, and re-layouts  111 us
    dot_general x32, matrix products, dot_t(): lax.dot_general(left_side, right_side, (((1,), (1,)), ((), ())), preferre...  97.3 us
    dot_general x16, matrix products, block_forward(): gate_up = jnp.dot(normed_ffn, w_gate_up, preferred_element_type=jnp.float32)  92.9 us
  transfers between devices with their start and end apart: 23, of which 12 were waited for; matrix products, arithmetic and copies ran while one was open for 2% of the time, Pallas kernels for 0%

commit v1 on v0

v1 whole, which is shorter than its diff:
```python
import functools

import jax
import jax.numpy as jnp
import numpy as np
from jax import lax
from jax.experimental import pallas as pl
from jax.experimental.pallas import tpu as pltpu
from jax.sharding import PartitionSpec as P

HEADS = 15
KV_HEADS = 5
HEAD_DIM = 64
FF = 2560
D = 960
Q_WIDTH = 960
QKV_WIDTH = 1600
SHORT_LEN = 16
LONG_LEN = 64
EPS = 1e-05
BASE = 10000.0
NEG = -1e30

BF = jnp.bfloat16
F32 = jnp.float32
MICROS = 2
ROWS = MICROS * LONG_LEN
CHUNK = 256
TILE = 128
TILES = 8
K_HALF = 15
V_HALF = 20
MESH = pl.DeviceIdType.MESH

KEEP = {"x": (0, 1024), "mid": (1024, 1024), "p": (2048, 1024), "qkv": (3072, 1664)}
KEEP["A"] = (4736, FF)
KEEP["B"] = (7296, FF)
KEEP_WIDTH = 9856
LEFT = {"n1": D, "mix": D, "n2": D, "hid": FF}
RIGHT = {"gqkv": QKV_WIDTH, "gat": D, "ggu": 2 * FF, "gff": D}
WEIGHTS = {"qkv": (D, QKV_WIDTH), "out": (Q_WIDTH, D), "gu": (D, 2 * FF), "dn": (FF, D)}


def nn(a, b):
    return lax.dot_general(a, b, (((1,), (0,)), ((), ())), preferred_element_type=F32)


def nt(a, b):
    return lax.dot_general(a, b, (((1,), (1,)), ((), ())), preferred_element_type=F32)


def tn(a, b):
    return lax.dot_general(a, b, (((0,), (0,)), ((), ())), preferred_element_type=F32)


def chunks(total, width=CHUNK):
    return [(c, min(width, total - c)) for c in range(0, total, width)]


def lane(rows):
    return lax.broadcasted_iota(jnp.int32, (rows, TILE), 1)


def inverse_rms(x):
    return lax.rsqrt(jnp.mean(x * x, -1, keepdims=True) + EPS)


def turn(tile):
    first = (lane(tile.shape[0]) % HEAD_DIM) < HEAD_DIM // 2
    return jnp.where(first, pltpu.roll(tile, TILE - 32, 1), pltpu.roll(tile, 32, 1))


def query_scale(column, rows):
    scale = HEAD_DIM**-0.5
    if column + TILE <= Q_WIDTH:
        return scale
    return jnp.where(lane(rows) < HEAD_DIM, scale, 1.0)


def head_pairs(ref, rows, first):
    low = lane(LONG_LEN) < HEAD_DIM
    tiles = {}
    spread = []
    for head in range(KV_HEADS):
        place = first + head
        t = place // 2
        if t not in tiles:
            width = min(TILE, QKV_WIDTH - t * TILE)
            x = ref[rows, t * TILE : t * TILE + width].astype(F32)
            if width < TILE:
                x = jnp.concatenate([x, x], 1)
            tiles[t] = (x, pltpu.roll(x, HEAD_DIM, 1))
        x, swapped = tiles[t]
        spread.append(jnp.where(low, x, swapped) if place % 2 == 0 else jnp.where(low, swapped, x))
    pairs = []
    for t in range(TILES):
        a = 2 * t // 3
        b = min((2 * t + 1) // 3, KV_HEADS - 1)
        pairs.append((spread[a] if a == b else jnp.where(low, spread[a], spread[b])).astype(BF))
    return pairs


def diagonal(ref, rows, t):
    low = lane(LONG_LEN) < HEAD_DIM
    x = ref[rows, t * TILE : (t + 1) * TILE].astype(F32)
    above = jnp.where(low, x, 0.0).astype(BF)
    below = jnp.where(low, 0.0, x).astype(BF)
    if t == TILES - 1:
        below = jnp.zeros_like(below)
    return jnp.concatenate([above, below], 0)


def micro_rows():
    return [slice(b * LONG_LEN, (b + 1) * LONG_LEN) for b in range(MICROS)]


def attention_forward(S):
    low = lane(LONG_LEN) < HEAD_DIM
    for rows in micro_rows():
        keys = head_pairs(S["qkv"], rows, K_HALF)
        for t in range(TILES):
            S["e"][rows, t * TILE : (t + 1) * TILE] = nt(keys[t], diagonal(S["qkv"], rows, t))
    for rows in micro_rows():
        bias = S["bias"][rows, :]
        for t in range(TILES):
            s = S["e"][rows, t * TILE : (t + 1) * TILE] + bias
            e = jnp.exp(s - jnp.max(s, 0, keepdims=True))
            z = 1.0 / jnp.sum(e, 0, keepdims=True)
            S["p"][rows, t * TILE : (t + 1) * TILE] = (e * z).astype(BF)
    for rows in micro_rows():
        values = head_pairs(S["qkv"], rows, V_HALF)
        for t in range(TILES):
            o = tn(S["p"][rows, t * TILE : (t + 1) * TILE], values[t])
            m = jnp.where(low, o[:LONG_LEN], o[LONG_LEN:]).astype(BF)
            width = min(TILE, Q_WIDTH - t * TILE)
            S["mix"][rows, t * TILE : t * TILE + width] = m[:, :width]


def block_forward(W, S, arrived):
    h = S["h"]
    x = h[...]
    S["x"][:, :D] = x.astype(BF)
    S["n1"][...] = (x * inverse_rms(x) * W["ga"][...]).astype(BF)
    arrived("qkv")
    n1 = S["n1"][...]
    for c, w in chunks(QKV_WIDTH):
        o = nn(n1, W["qkv"][:, c : c + w])
        for t, tw in chunks(w, TILE):
            column = c + t
            tile = o[:, t : t + tw]
            if column < Q_WIDTH + KV_HEADS * HEAD_DIM:
                tile = tile * S["cos"][...] + turn(tile) * S["sin"][...]
                if column < Q_WIDTH:
                    tile = tile * query_scale(column, ROWS)
            S["qkv"][:, column : column + tw] = tile.astype(BF)
    attention_forward(S)
    arrived("out")
    mix = S["mix"][...]
    for c, w in chunks(D):
        h[:, c : c + w] = h[:, c : c + w] + nn(mix, W["out"][:, c : c + w])
    x = h[...]
    S["mid"][:, :D] = x.astype(BF)
    S["n2"][...] = (x * inverse_rms(x) * W["gf"][...]).astype(BF)
    arrived("gu")
    n2 = S["n2"][...]
    for c, w in chunks(FF):
        gate = nn(n2, W["gu"][:, c : c + w])
        up = nn(n2, W["gu"][:, FF + c : FF + c + w])
        sg = 1.0 / (1.0 + jnp.exp(-gate))
        act = gate * sg
        S["B"][:, c : c + w] = act.astype(BF)
        S["A"][:, c : c + w] = (up * sg * (1.0 + gate * (1.0 - sg))).astype(BF)
        S["hid"][:, c : c + w] = (act * up).astype(BF)
    arrived("dn")
    hid = S["hid"][...]
    for c, w in chunks(D):
        h[:, c : c + w] = h[:, c : c + w] + nn(hid, W["dn"][:, c : c + w])


def attention_backward(S):
    low = lane(LONG_LEN) < HEAD_DIM
    for rows in micro_rows():
        values = head_pairs(S["qkv"], rows, V_HALF)
        for t in range(TILES):
            S["e"][rows, t * TILE : (t + 1) * TILE] = nt(values[t], diagonal(S["gm"], rows, t))
    for rows in micro_rows():
        for t in range(TILES):
            gp = S["e"][rows, t * TILE : (t + 1) * TILE]
            p = S["p"][rows, t * TILE : (t + 1) * TILE].astype(F32)
            total = jnp.sum(gp * p, 0, keepdims=True)
            S["gs"][rows, t * TILE : (t + 1) * TILE] = (p * (gp - total)).astype(BF)

    def store(rows, column, value, turned):
        if turned:
            value = value * S["cos"][rows, :] - turn(value) * S["sin"][rows, :]
        width = min(TILE, QKV_WIDTH - column)
        S["gqkv"][rows, column : column + width] = value[:, :width].astype(BF)

    def fold(parts):
        sums = []
        for head in range(KV_HEADS):
            lower, upper = None, None
            for q in (3 * head, 3 * head + 1, 3 * head + 2):
                part = parts[q // 2]
                if q % 2 == 0:
                    lower = part if lower is None else lower + part
                else:
                    upper = part if upper is None else upper + part
            sums.append((jnp.where(low, lower, 0.0), jnp.where(low, 0.0, upper)))
        return sums

    def placed(sums, head, half):
        lower, upper = sums[head]
        if half == 0:
            return lower + pltpu.roll(upper, HEAD_DIM, 1)
        return upper + pltpu.roll(lower, HEAD_DIM, 1)

    for rows in micro_rows():
        keys = head_pairs(S["qkv"], rows, K_HALF)
        grad_k, grad_v = [], []
        last = None
        for t in range(TILES):
            gs = S["gs"][rows, t * TILE : (t + 1) * TILE]
            grad_k.append(nn(gs, diagonal(S["qkv"], rows, t)))
            grad_v.append(
                nn(S["p"][rows, t * TILE : (t + 1) * TILE], diagonal(S["gm"], rows, t))
            )
            o = tn(gs, keys[t])
            grad_q = jnp.where(low, o[:LONG_LEN], o[LONG_LEN:]) * HEAD_DIM**-0.5
            if t < TILES - 1:
                store(rows, t * TILE, grad_q, True)
            else:
                last = grad_q
        k, v = fold(grad_k), fold(grad_v)
        store(rows, 896, jnp.where(low, last, placed(k, 0, 1)), True)
        store(rows, 1024, placed(k, 1, 0) + placed(k, 2, 1), True)
        store(rows, 1152, placed(k, 3, 0) + placed(k, 4, 1), True)
        store(rows, 1280, placed(v, 0, 0) + placed(v, 1, 1), False)
        store(rows, 1408, placed(v, 2, 0) + placed(v, 3, 1), False)
        store(rows, 1536, placed(v, 4, 0), False)


def rms_backward(x, gain, e, base):
    r = inverse_rms(x)
    scaled = e * gain
    mean = jnp.mean(x * scaled, -1, keepdims=True)
    return base + r * scaled - x * (r * r * r * mean), jnp.sum(e * x * r, 0, keepdims=True)


def block_backward(W, S, gain_attn_grad, gain_ffn_grad):
    g = S["h"]
    S["gff"][...] = g[...].astype(BF)
    gff = S["gff"][...]
    for c, w in chunks(FF):
        gh = nn(gff, W["dnT"][:, c : c + w])
        S["ggu"][:, c : c + w] = (gh * S["A"][:, c : c + w].astype(F32)).astype(BF)
        S["ggu"][:, FF + c : FF + c + w] = (gh * S["B"][:, c : c + w].astype(F32)).astype(BF)
    ggu = S["ggu"][...]
    for c, w in chunks(D):
        S["e"][:, c : c + w] = nn(ggu, W["guT"][:, c : c + w])
    new, gain = rms_backward(S["mid"][:, :D].astype(F32), W["gf"][...], S["e"][:, :D], g[...])
    gain_ffn_grad[...] += gain
    g[...] = new
    S["gat"][...] = new.astype(BF)
    gat = S["gat"][...]
    for c, w in chunks(Q_WIDTH):
        S["gm"][:, c : c + w] = nn(gat, W["outT"][:, c : c + w]).astype(BF)
    attention_backward(S)
    gqkv = S["gqkv"][...]
    for c, w in chunks(D):
        S["e"][:, c : c + w] = nn(gqkv, W["qkvT"][:, c : c + w])
    new, gain = rms_backward(S["x"][:, :D].astype(F32), W["ga"][...], S["e"][:, :D], g[...])
    gain_attn_grad[...] += gain
    g[...] = new


def transpose_weights(W):
    row = lax.broadcasted_iota(jnp.int32, (CHUNK, CHUNK), 0)
    column = lax.broadcasted_iota(jnp.int32, (CHUNK, CHUNK), 1)
    unit = jnp.where(row == column, 1.0, 0.0).astype(BF)
    for name, (depth, width) in WEIGHTS.items():
        source, target = W[name], W[name + "T"]

        def strip(start, size, source=source, target=target, depth=depth):
            for k, kw in chunks(depth):
                tile = nt(unit[:size, :size], source[k : k + kw, pl.ds(start, size)])
                target[pl.ds(start, size), k : k + kw] = tile.astype(BF)

        whole = width // CHUNK

        def one(i, carry, strip=strip):
            strip(pl.multiple_of(i * CHUNK, CHUNK), CHUNK)
            return carry

        lax.fori_loop(0, whole, one, 0)
        if width % CHUNK:
            strip(whole * CHUNK, width % CHUNK)


def make_constants(S, meta, item, tables):
    cos_long, sin_long, cos_short, sin_short = tables
    shape = (LONG_LEN, TILE)
    slot = lax.broadcasted_iota(jnp.int32, shape, 0)
    other = lane(LONG_LEN) % LONG_LEN
    piece = (slot // SHORT_LEN).astype(F32)
    other_piece = (other // SHORT_LEN).astype(F32)
    for b, rows in enumerate(micro_rows()):
        is_long = jnp.broadcast_to(meta[item, b : b + 1, :], shape) > 0.5
        count = jnp.broadcast_to(meta[item, MICROS + b : MICROS + b + 1, :], shape)
        S["cos"][rows, :] = jnp.where(is_long, cos_long[...], cos_short[...])
        S["sin"][rows, :] = jnp.where(is_long, sin_long[...], sin_short[...])
        short = jnp.where(other_piece < count, 0.0, jnp.where(slot == other, 0.0, NEG))
        short = jnp.where(piece == other_piece, short, NEG)
        bias = jnp.where(is_long, 0.0, short)
        S["bias"][rows, :] = jnp.where(slot <= other, bias, NEG)
        S["valid"][rows, :] = jnp.where(is_long, 1.0, jnp.where(piece < count, 1.0, 0.0))


IN_NAMES = (
    ["tok", "cot", "meta", "ga", "gf"] + list(WEIGHTS) + ["cosl", "sinl", "coss", "sins"]
)
OUT_NAMES = ["out", "gin"] + list(LEFT) + list(RIGHT) + ["keep", "gga", "ggf"]


def pipeline_kernel(sections, chips, own, scratch_names, *refs):
    refs = list(refs)
    I = dict(zip(IN_NAMES, refs))
    O = dict(zip(OUT_NAMES, refs[len(IN_NAMES) :]))
    R = dict(zip(scratch_names, refs[len(IN_NAMES) + len(OUT_NAMES) :]))
    far = own * (chips - 1)
    section = lax.axis_index("section")
    data = lax.axis_index("dp")
    chip, core = data // 2, data % 2
    is_first, is_last = section == 0, section == sections - 1
    W = {name: R["w_" + name] for name in WEIGHTS}
    W.update({name + "T": R["t_" + name] for name in WEIGHTS})
    W["ga"], W["gf"] = I["ga"], I["gf"]

    def partner(d):
        return lax.rem(chip - d + chips, chips) * 2 + core

    barrier = pltpu.get_barrier_semaphore()

    @pl.when(section > 0)
    def _():
        pl.semaphore_signal(barrier, 1, device_id={"section": section - 1}, device_id_type=MESH)

    @pl.when(section < sections - 1)
    def _():
        pl.semaphore_signal(barrier, 1, device_id={"section": section + 1}, device_id_type=MESH)

    for d in range(1, chips):
        pl.semaphore_signal(barrier, 1, device_id={"dp": partner(d)}, device_id_type=MESH)

    weight_copies = {
        name: pltpu.make_async_copy(I[name], W[name], R["w_sem"].at[k])
        for k, name in enumerate(WEIGHTS)
    }
    for copy in weight_copies.values():
        copy.start()

    def rows_of(ref, j):
        return ref.at[pl.ds(pl.multiple_of(j * ROWS, ROWS), ROWS), :]

    def token_copy(j):
        return pltpu.make_async_copy(rows_of(I["tok"], j), R["fin"].at[j], R["f_sem"].at[j])

    def cotangent_copy(j):
        return pltpu.make_async_copy(rows_of(I["cot"], j), R["bin"].at[j], R["b_sem"].at[j])

    @pl.when(is_first)
    def _():
        for j in range(own):
            token_copy(j).start()

    @pl.when(is_last)
    def _():
        for j in range(own):
            cotangent_copy(j).start()

    R["meta"][0:own] = I["meta"][...]
    O["gga"][...] = jnp.zeros_like(O["gga"])
    O["ggf"][...] = jnp.zeros_like(O["ggf"])
    R["gm"][...] = jnp.zeros_like(R["gm"])

    others = chips - 1
    near = jnp.where(is_first, 0, 1) + jnp.where(is_last, 0, 1)
    pl.semaphore_wait(barrier, near + others)

    def meta_copy(d):
        return pltpu.make_async_remote_copy(
            src_ref=I["meta"],
            dst_ref=R["meta"].at[pl.ds(own * d, own)],
            send_sem=R["ms_sem"].at[d - 1],
            recv_sem=R["m_sem"].at[d - 1],
            device_id={"dp": partner(d)},
            device_id_type=MESH,
        )

    def next_copy(j):
        return pltpu.make_async_remote_copy(
            src_ref=R["outs"].at[j],
            dst_ref=R["fin"].at[j],
            send_sem=R["fs_sem"].at[j],
            recv_sem=R["f_sem"].at[j],
            device_id={"section": section + 1},
            device_id_type=MESH,
        )

    def previous_copy(j):
        return pltpu.make_async_remote_copy(
            src_ref=R["outs"].at[j],
            dst_ref=R["bin"].at[j],
            send_sem=R["bs_sem"].at[j],
            recv_sem=R["b_sem"].at[j],
            device_id={"section": section - 1},
            device_id_type=MESH,
        )

    def far_copy(buffer, recv, send, d, j):
        return pltpu.make_async_remote_copy(
            src_ref=R[buffer].at[j],
            dst_ref=R[buffer].at[own * d + j],
            send_sem=R[send].at[own * (d - 1) + j],
            recv_sem=R[recv].at[own * d + j],
            device_id={"dp": partner(d)},
            device_id_type=MESH,
        )

    def far_forward(d, j):
        return far_copy("fin", "f_sem", "fx_sem", d, j)

    def far_backward(d, j):
        return far_copy("bin", "b_sem", "bx_sem", d, j)

    def out_copy(j):
        return pltpu.make_async_copy(R["outs"].at[j], rows_of(O["out"], j), R["o_sem"].at[j])

    def grad_copy(j):
        return pltpu.make_async_copy(R["outs"].at[j], rows_of(O["gin"], j), R["g_sem"].at[j])

    for d in range(1, chips):
        meta_copy(d).start()

    early = section >= sections // 2

    def views(slot):
        S = {name: R[name] for name in ("h", "e", "gm", "gs", "cos", "sin", "bias", "valid")}
        for name, (start, width) in KEEP.items():
            S[name] = R["keep"].at[slot, :, start : start + width]
        for name in list(LEFT) + list(RIGHT):
            S[name] = R[name].at[slot]
        return S

    def left_copies(slot, index):
        pairs = [(R["keep"].at[slot], O["keep"].at[index])]
        pairs += [(R[name].at[slot], O[name].at[index]) for name in LEFT]
        return [
            pltpu.make_async_copy(a, b, R["l_sem"].at[slot, k]) for k, (a, b) in enumerate(pairs)
        ]

    def right_copies(slot, index):
        return [
            pltpu.make_async_copy(R[name].at[slot], O[name].at[index], R["r_sem"].at[slot, k])
            for k, name in enumerate(RIGHT)
        ]

    def keep_load(slot, index):
        return pltpu.make_async_copy(O["keep"].at[index], R["keep"].at[slot], R["k_sem"].at[slot])

    def forward_phase(start, count, is_far):
        def step(k, carry):
            item = start + k

            @pl.when(is_far)
            def _():
                d = item // own
                far_copy("fin", "f_sem", "fx_sem", d, item - own * d).wait_recv()

            @pl.when(jnp.logical_not(is_far))
            def _():
                @pl.when(is_first)
                def _():
                    token_copy(item).wait()

                @pl.when(jnp.logical_not(is_first))
                def _():
                    next_copy(item).wait_recv()

                for d in range(1, chips):
                    far_forward(d, item).start()

            make_constants(
                R, R["meta"], item, (I["cosl"], I["sinl"], I["coss"], I["sins"])
            )
            R["h"][...] = R["fin"][item].astype(F32)

            def one(f, carry):
                @pl.when(k > 0)
                def _():
                    for copy in left_copies(f, 2 * (item - 1) + f):
                        copy.wait()

                fresh = jnp.logical_not(early) & (item == 0) & (f == 0)

                def arrived(name):
                    @pl.when(fresh)
                    def _():
                        weight_copies[name].wait()

                block_forward(W, views(f), arrived)
                for copy in left_copies(f, 2 * item + f):
                    copy.start()
                return carry

            lax.fori_loop(0, 2, one, 0)

            @pl.when(jnp.logical_not(is_far))
            def _():
                R["outs"][item] = (R["h"][...] * R["valid"][:, 0:1]).astype(BF)

                @pl.when(jnp.logical_not(is_last))
                def _():
                    next_copy(item).start()

                out_copy(item).start()

            return carry

        lax.fori_loop(0, count, step, 0)
        for f in range(2):
            for copy in left_copies(f, 2 * (start + count - 1) + f):
                copy.wait()

    def backward_phase(start, count, is_far):
        keep_load(1, 2 * start + 1).start()

        def step(k, carry):
            item = start + k

            @pl.when(is_far)
            def _():
                d = item // own
                far_copy("bin", "b_sem", "bx_sem", d, item - own * d).wait_recv()

            @pl.when(jnp.logical_not(is_far))
            def _():
                @pl.when(is_last)
                def _():
                    cotangent_copy(item).wait()

                @pl.when(jnp.logical_not(is_last))
                def _():
                    previous_copy(item).wait_recv()

                for d in range(1, chips):
                    far_backward(d, item).start()

            make_constants(
                R, R["meta"], item, (I["cosl"], I["sinl"], I["coss"], I["sins"])
            )
            R["h"][...] = R["bin"][item].astype(F32) * R["valid"][:, 0:1]

            def one(i, carry):
                f = 1 - i
                keep_load(f, 2 * item + f).wait()

                @pl.when(f == 1)
                def _():
                    keep_load(0, 2 * item).start()

                @pl.when((f == 0) & (k < count - 1))
                def _():
                    keep_load(1, 2 * item + 3).start()

                @pl.when(k > 0)
                def _():
                    for copy in right_copies(f, 2 * (item - 1) + f):
                        copy.wait()

                block_backward(W, views(f), O["gga"], O["ggf"])
                for copy in right_copies(f, 2 * item + f):
                    copy.start()
                return carry

            lax.fori_loop(0, 2, one, 0)

            @pl.when(jnp.logical_not(is_far))
            def _():
                @pl.when(jnp.logical_not(is_last))
                def _():
                    next_copy(item).wait_send()

                out_copy(item).wait()
                R["outs"][item] = R["h"][...].astype(BF)

                @pl.when(jnp.logical_not(is_first))
                def _():
                    previous_copy(item).start()

                grad_copy(item).start()

            return carry

        lax.fori_loop(0, count, step, 0)
        for f in range(2):
            for copy in right_copies(f, 2 * (start + count - 1) + f):
                copy.wait()

    phases = 4 if far else 2

    def phase(p, carry):
        if far:
            is_far = jnp.where(is_last, p >= 2, lax.rem(p, 2) == 1)
            is_back = jnp.where(is_last, lax.rem(p, 2) == 1, p >= 2)
            start = jnp.where(is_far, own, 0)
            count = jnp.where(is_far, far, own)
        else:
            is_far, is_back, start, count = p < 0, p == 1, 0, own

        @pl.when((p == 0) & early)
        def _():
            for copy in weight_copies.values():
                copy.wait()

        @pl.when(jnp.where(early, p == 0, p == phases // 2))
        def _():
            transpose_weights(W)

        if far:

            @pl.when(is_far & jnp.logical_not(is_back))
            def _():
                for d in range(1, chips):
                    meta_copy(d).wait_recv()

        @pl.when(jnp.logical_not(is_back))
        def _():
            forward_phase(start, count, is_far)

        @pl.when(is_back)
        def _():
            backward_phase(start, count, is_far)

        return carry

    lax.fori_loop(0, phases, phase, 0)

    for j in range(own):

        @pl.when(jnp.logical_not(is_first))
        def _():
            previous_copy(j).wait_send()

        grad_copy(j).wait()
        for d in range(1, chips):
            far_forward(d, j).wait_send()
            far_backward(d, j).wait_send()
    for d in range(1, chips):
        meta_copy(d).wait_send()


def rotary_tables():
    half = HEAD_DIM // 2
    frequency = BASE ** (-2.0 * np.arange(half, dtype=np.float32) / HEAD_DIM)
    slots = np.arange(LONG_LEN)
    tables = []
    for position in (slots, slots % SHORT_LEN):
        angle = position.astype(np.float32)[:, None] * frequency[None, :].astype(np.float32)
        cos, sin = np.cos(angle), np.sin(angle)
        tables.append(np.tile(np.concatenate([cos, cos], 1), (1, 2)).astype(np.float32))
        tables.append(np.tile(np.concatenate([-sin, sin], 1), (1, 2)).astype(np.float32))
    return tables


def run_pipeline(sections, chips, own, *args):
    items = own * chips
    vmem = lambda *shape, dtype=BF: pltpu.VMEM(shape, dtype)
    scratch = {
        "fin": vmem(items, ROWS, D),
        "bin": vmem(items, ROWS, D),
        "outs": vmem(own, ROWS, D),
        "meta": vmem(items, 8, TILE, dtype=F32),
        "keep": vmem(2, ROWS, KEEP_WIDTH),
        "h": vmem(ROWS, D, dtype=F32),
        "e": vmem(ROWS, 1024, dtype=F32),
        "gm": vmem(ROWS, 1024),
        "gs": vmem(ROWS, 1024),
    }
    for name in ("cos", "sin", "bias", "valid"):
        scratch[name] = vmem(ROWS, TILE, dtype=F32)
    for name, width in {**LEFT, **RIGHT}.items():
        scratch[name] = vmem(2, ROWS, width)
    for name, (depth, width) in WEIGHTS.items():
        scratch["w_" + name] = vmem(depth, width)
        scratch["t_" + name] = vmem(width, depth)
    far = max(1, own * (chips - 1))
    counts = {
        "w_sem": (len(WEIGHTS),),
        "f_sem": (items,),
        "b_sem": (items,),
        "fs_sem": (own,),
        "bs_sem": (own,),
        "fx_sem": (far,),
        "bx_sem": (far,),
        "m_sem": (max(1, chips - 1),),
        "ms_sem": (max(1, chips - 1),),
        "o_sem": (own,),
        "g_sem": (own,),
        "l_sem": (2, 1 + len(LEFT)),
        "r_sem": (2, len(RIGHT)),
        "k_sem": (2,),
    }
    for name, shape in counts.items():
        scratch[name] = pltpu.SemaphoreType.DMA(shape)
    hbm, local = pl.BlockSpec(memory_space=pl.ANY), pl.BlockSpec(memory_space=pltpu.VMEM)
    shapes = {"out": (own * ROWS, D), "gin": (own * ROWS, D)}
    for name, width in {**LEFT, **RIGHT}.items():
        shapes[name] = (2 * items, ROWS, width)
    shapes["keep"] = (2 * items, ROWS, KEEP_WIDTH)
    out_shape = [jax.ShapeDtypeStruct(shapes[name], BF) for name in OUT_NAMES[:-2]]
    out_shape += [jax.ShapeDtypeStruct((1, D), F32)] * 2
    in_vmem = ("meta", "ga", "gf", "cosl", "sinl", "coss", "sins")
    return pl.pallas_call(
        functools.partial(pipeline_kernel, sections, chips, own, list(scratch)),
        out_shape=out_shape,
        in_specs=[local if name in in_vmem else hbm for name in IN_NAMES],
        out_specs=[hbm] * (len(OUT_NAMES) - 2) + [local] * 2,
        scratch_shapes=list(scratch.values()),
        compiler_params=pltpu.CompilerParams(
            collective_id=0, has_side_effects=True, vmem_limit_bytes=127 * 2**19
        ),
    )(*args)


def body(tokens, cotangent, seq_counts, attn_gain, w_qkv, w_out, ffn_gain, w_gate_up, w_down):
    sections = lax.axis_size("section")
    groups = lax.axis_size("dp")
    data = lax.axis_index("dp")
    chips = groups // 2
    own = tokens.shape[0] // ROWS
    meta = seq_counts.astype(F32).reshape(own, MICROS, 2).transpose(0, 2, 1)
    meta = jnp.pad(meta.reshape(own, 2 * MICROS), ((0, 0), (0, 8 - 2 * MICROS)))
    meta = jnp.broadcast_to(meta[:, :, None], (own, 8, TILE))
    results = run_pipeline(
        sections,
        chips,
        own,
        tokens,
        cotangent,
        meta,
        attn_gain,
        ffn_gain,
        w_qkv[0],
        w_out[0],
        w_gate_up[0],
        w_down[0],
        *[jnp.asarray(table) for table in rotary_tables()],
    )
    O = dict(zip(OUT_NAMES, results))
    share = D // groups
    begin = (data // 2) * 2 * share
    flip = [(i, i ^ 1) for i in range(groups)]

    def flat(name):
        return O[name].reshape(-1, O[name].shape[-1])

    def part(value, axis=1):
        return lax.dynamic_slice_in_dim(value, begin, 2 * share, axis)

    def exchange(both, axis):
        mine = lax.dynamic_slice_in_dim(both, (data % 2) * share, share, axis)
        other = lax.dynamic_slice_in_dim(both, (1 - data % 2) * share, share, axis)
        return mine + lax.ppermute(other.astype(BF), "dp", flip).astype(F32)

    gate_up_grad = exchange(tn(part(flat("n2")), flat("ggu")), 0)
    down_grad = exchange(tn(flat("hid"), part(flat("gff"))), 1)
    qkv_grad = exchange(tn(part(flat("n1")), flat("gqkv")), 0)
    out_grad = exchange(tn(flat("mix"), part(flat("gat"))), 1)
    attn_gain_grad = exchange(part(O["gga"]), 1)
    ffn_gain_grad = exchange(part(O["ggf"]), 1)
    return (
        O["out"][None],
        O["gin"][None],
        attn_gain_grad,
        qkv_grad[None],
        out_grad[None],
        ffn_gain_grad,
        gate_up_grad[None],
        down_grad[None],
    )


def solution(mesh):
    in_specs = (
        P("dp", None),
        P("dp", None),
        P("dp", None),
        P("section", None),
        P("section", None, None),
        P("section", None, None),
        P("section", None),
        P("section", None, None),
        P("section", None, None),
    )
    out_specs = (
        P("section", "dp", None),
        P("section", "dp", None),
        P("section", "dp"),
        P("section", "dp", None),
        P("section", None, "dp"),
        P("section", "dp"),
        P("section", "dp", None),
        P("section", None, "dp"),
    )
    return jax.shard_map(body, mesh=mesh, in_specs=in_specs, out_specs=out_specs, check_vma=False)
```

time: 3350 us -> 356 us (0.11)
  waiting for transfers between devices: 1760 us -> 0.02 us
  local copies, waits for them, and re-layouts: 525 us -> 26.2 us
  matrix products: 450 us -> 19.3 us
  Pallas kernels: 0 us -> 291 us
  starting transfers between devices: 275 us -> 1.38 us
  other arithmetic: 241 us -> 17 us
  loops' own time: 56.8 us -> 0 us
    ppermute x22 -> x6, waiting for transfers between devices: 1440 us -> 0.02 us  [exchange(): return mine + lax.ppermute(other.astype(BF), 'dp', flip).astype(F32)]
    dot_general x168 -> x4, matrix products: 450 us -> 19.3 us  [tn(): lax.dot_general(a, b, (((0,), (0,)), ((), ())), preferred_element_type=F32)]
    psum x1 -> x0, waiting for transfers between devices: 328 us -> none  [body(): lax.psum(grad_qkv.astype(jnp.bfloat16), 'dp').astype(jnp.float32)]
    pallas_call x0 -> x1, Pallas kernels: none -> 291 us  [run_pipeline(): pl.pallas_call(functools.partial(pipeline_kernel, sections, chips, own, l...]
    ppermute x22 -> x6, starting transfers between devices: 275 us -> 1.38 us  [exchange(): return mine + lax.ppermute(other.astype(BF), 'dp', flip).astype(F32)]
    slice x126 -> x0, local copies, waits for them, and re-layouts: 149 us -> none  [the longest x32 52.9 us: block_forward(): qkv_proj[:, q_width:q_width + kv_width]]
    cond x704 -> x0, local copies, waits for them, and re-layouts: 111 us -> none
    convert_element_type x101 -> x1, other arithmetic: 87.7 us -> 0.68 us  [body(): meta = seq_counts.astype(F32).reshape(own, MICROS, 2).transpose(0, 2, 1)]
  transfers between devices with their start and end apart: 23 -> 6, of which waited for: 12 -> 0; matrix products, arithmetic and copies ran while one was open for 2% -> 11% of each run, Pallas kernels for 0% -> 0%
where the time goes in v1:
time: 356 us
  Pallas kernels  291 us (82%)
  local copies, waits for them, and re-layouts  26.2 us (7%)
  matrix products  19.3 us (5%)
  other arithmetic  17 us (5%)
    pallas_call x1, Pallas kernels, run_pipeline(): pl.pallas_call(functools.partial(pipeline_kernel, sections, chips, own, l...  291 us
    unnamed x29, local copies, waits for them, and re-layouts  20.8 us
    dot_general x4, matrix products, tn(): lax.dot_general(a, b, (((0,), (0,)), ((), ())), preferred_element_type=F32)  19.3 us
  transfers between devices with their start and end apart: 6, of which 0 were waited for; matrix products, arithmetic and copies ran while one was open for 11% of the time, Pallas kernels for 0%

profile of v1, /device:TPU:0, one launch (start us, length us, event | category | flops | bytes accessed | tf_op | source)
XLA Modules:
  0.0 355.7 jit_solution(6682234650169116620)
XLA Ops:
  0.6 2.0 copy.23.refs_0_
  2.7 2.0 copy.24.refs_1_
  4.7 0.7 convert_element_type.41
  5.4 0.1 reshape.47
  5.5 0.1 reshape.48
  5.6 7.9 %copy.22 = bf16[1,2560,960]{2,1,0:T(8,128)(2,1)} copy(bf16[1,2560,960]{1,2,0:T(8,128)(2,1)} %param.21) | data formatting | bytes 9830400 | tf_op args[8]
  13.4 0.7 broadcast_in_dim.24.refs_2_
  14.1 290.9 %shard_map.188 = (bf16[256,960]{1,0:T(8,128)(2,1)}, bf16[256,960]{1,0:T(8,128)(2,1)}, bf16[8,128,960]{2,1,0:T(8,128)(2,1)}, bf16[8,128,960]{2,1,0:T(8,128)(2,1)}...) custom-call(bf16[256,960]{1,0:T(8,128)(2,1)} %copy.23.refs_0_, ...), custom_call_target="tpu_custom_call" | custom-call | tf_op jit(solution)/shard_map/pallas_call | solution.py:724
  305.0 0.7 fusion.13
  305.8 4.6 %fusion.6 = f32[480,1600]{1,0:T(8,128)S(1)} fusion(bf16[1024,1600]{1,0:T(8,128)(2,1)} %bitcast.41, bf16[1024,960]{1,0:T(8,128)(2,1)} %bitcast.45, s32[]{:T(128)S(6)} %select_n.67), kind=kOutput, calls=%fused_computation.12 | convolution fusion | flops 1572864000 | bytes 7528452 | tf_op jit(solution)/shard_map/dot_general | solution.py:53
  310.4 1.1 dynamic-slice_convert_fusion.2
  311.5 0.5 collective-permute-start.1
  312.0 2.8 fusion.4
  314.8 1.2 dynamic-slice_convert_fusion.3
  316.0 0.2 collective-permute-start.2
  316.3 0.4 collective-permute-start.3
  316.7 5.5 %fusion.2 = f32[480,5120]{1,0:T(8,128)S(1)} fusion(bf16[1024,5120]{1,0:T(8,128)(2,1)S(1)} %bitcast.32, bf16[1024,960]{1,0:T(8,128)(2,1)S(1)} %bitcast.36, s32[]{:T(128)S(6)} %select_n.67), kind=kOutput, calls=%fused_computation.8 | convolution fusion | flops 5033164800 | bytes 21364740 | tf_op jit(solution)/shard_map/dot_general | solution.py:53
  322.2 0.3 dynamic-slice_convert_fusion
  322.5 0.2 collective-permute-start.4
  322.8 2.6 copy-done.7
  325.3 6.3 %fusion = f32[2560,480]{0,1:T(8,128)S(1)} fusion(bf16[1024,2560]{1,0:T(8,128)(2,1)} %bitcast.40, bf16[1024,960]{1,0:T(8,128)(2,1)S(1)} %bitcast.42, s32[]{:T(128)S(6)} %select_n.67), kind=kOutput, calls=%fused_computation.6 | convolution fusion | flops 2516582400 | bytes 11206660 | tf_op jit(solution)/shard_map/dot_general | solution.py:53
  331.7 2.2 copy-done.2
  333.9 1.2 dynamic-slice_convert_fusion.1
  335.1 2.0 copy.25
  337.1 2.0 copy.26
  339.1 0.1 collective-permute-start.5
  339.3 1.3 fusion.12
  340.5 0.6 fusion.14
  341.2 2.8 add_bitcast_fusion.3
  344.0 2.8 add_bitcast_fusion.2
  346.8 4.2 %add_bitcast_fusion.1 = f32[1,2560,240]{1,2,0:T(8,128)} fusion(bf16[2560,240]{0,1:T(8,128)(2,1)S(1)} %collective-permute-done.5, f32[2560,480]{0,1:T(8,128)} %copy-done.2, s32[]{:T(128)S(6)} %select_n.64), kind=kLoop, calls=%fused_computation.2 | loop fusion | flops 1228800 | bytes 6144004 | tf_op jit(solution)/shard_map/broadcast_in_dim | solution.py:790
  351.1 4.6 %add_bitcast_fusion = f32[1,240,5120]{2,1,0:T(8,128)} fusion(bf16[240,5120]{1,0:T(8,128)(2,1)} %collective-permute-done.4, f32[480,5120]{1,0:T(8,128)S(1)} %copy-done.1, s32[]{:T(128)S(6)} %select_n.64), kind=kLoop, calls=%fused_computation | loop fusion | flops 2457600 | bytes 12288004 | tf_op jit(solution)/shard_map/broadcast_in_dim | solution.py:789
  (33 shorter events, 0.2 us)
Async XLA Ops:
  305.7 33.4 %collective-permute-start = (bf16[1,240]{1,0:T(2,128)(2,1)S(1)}, bf16[1,240]{1,0:T(2,128)(2,1)S(1)}, u32[]{:S(2)}, u32[]{:S(2)}) collective-permute-start(bf16[1,240]{1,0:T(2,128)(2,1)S(1)} %fusion.13), channel_id=1, source_target_pairs={{0,1},{1,0},{2,3},{3,2},{4,5},{5,4},{6,7},{7,6},{8,9},{9,8},{10,11... | collective-permute-start | bytes 1448 | tf_op jit(solution)/shard_map/ppermute | solution.py:774
  305.8 6.2 %copy-start.8 = (bf16[8,128,960]{2,1,0:T(8,128)(2,1)S(1)}, bf16[8,128,960]{2,1,0:T(8,128)(2,1)}, u32[]{:S(2)}) copy-start(bf16[8,128,960]{2,1,0:T(8,128)(2,1)} %get-tuple-element.25) | copy-start | bytes 5898244
  305.8 10.9 %slice-start = ((s8[10485760]{0:T(1024)(128)(4,1)}), s8[4194304]{0:T(1024)(128)(4,1)S(1)}, s32[]{:S(2)}) async-start(s8[10485760]{0:T(1024)(128)(4,1)} %bitcast.30), calls=%async_computation | async-start | bytes 8388608
  305.8 10.9 %slice-start.1 = ((s8[10485760]{0:T(1024)(128)(4,1)}), s8[4194304]{0:T(1024)(128)(4,1)S(1)}, s32[]{:S(2)}) async-start(s8[10485760]{0:T(1024)(128)(4,1)} %bitcast.30), calls=%async_computation.1 | async-start | bytes 8388608
  310.4 4.4 %copy-start.3 = (f32[480,1600]{1,0:T(8,128)}, f32[480,1600]{1,0:T(8,128)S(1)}, u32[]{:S(2)}) copy-start(f32[480,1600]{1,0:T(8,128)S(1)} %fusion.6) | copy-start | bytes 9216004
  311.5 32.5 %collective-permute-start.1 = (bf16[240,1600]{1,0:T(8,128)(2,1)}, bf16[240,1600]{1,0:T(8,128)(2,1)S(1)}, u32[]{:S(2)}, u32[]{:S(2)}) collective-permute-start(bf16[240,1600]{1,0:T(8,128)(2,1)} %dynamic-slice_convert_fusion.2), channel_id=1, source_target_pairs={{0,1},{1,0},{2,3},{3,2},{4,5},{5,4},{6,7},{7,6},{8,9},{9,8},{10,11... | collective-permute-start | bytes 2304008 | tf_op jit(solution)/shard_map/ppermute | solution.py:774
  312.0 4.2 %copy-start.6 = (f32[1,960]{1,0:T(1,128)S(1)}, f32[1,960]{1,0:T(1,128)}, u32[]{:S(2)}) copy-start(f32[1,960]{1,0:T(1,128)} %get-tuple-element.27) | copy-start | bytes 11524
  312.0 4.6 %slice-start.2 = ((s8[10485760]{0:T(1024)(128)(4,1)}), s8[2097152]{0:T(1024)(128)(4,1)S(1)}, s32[]{:S(2)}) async-start(s8[10485760]{0:T(1024)(128)(4,1)} %bitcast.30), calls=%async_computation.2 | async-start | bytes 4194304
  312.0 4.6 %copy-start.5 = (bf16[8,128,960]{2,1,0:T(8,128)(2,1)S(1)}, bf16[8,128,960]{2,1,0:T(8,128)(2,1)}, u32[]{:S(2)}) copy-start(bf16[8,128,960]{2,1,0:T(8,128)(2,1)} %get-tuple-element.28) | copy-start | bytes 5898244
  314.8 1.8 copy-start.4
  316.0 25.1 %collective-permute-start.2 = (bf16[960,240]{1,0:T(8,128)(2,1)}, bf16[960,240]{1,0:T(8,128)(2,1)}, u32[]{:S(2)}, u32[]{:S(2)}) collective-permute-start(bf16[960,240]{1,0:T(8,128)(2,1)} %dynamic-slice_convert_fusion.3), channel_id=1, source_target_pairs={{0,1},{1,0},{2,3},{3,2},{4,5},{5,4},{6,7},{7,6},{8,9},{9,8},{10,11... | collective-permute-start | bytes 1382408 | tf_op jit(solution)/shard_map/ppermute | solution.py:774
  316.3 24.3 %collective-permute-start.3 = (bf16[1,240]{1,0:T(2,128)(2,1)S(1)}, bf16[1,240]{1,0:T(2,128)(2,1)S(1)}, u32[]{:S(2)}, u32[]{:S(2)}) collective-permute-start(bf16[1,240]{1,0:T(2,128)(2,1)S(1)} %fusion.15), channel_id=1, source_target_pairs={{0,1},{1,0},{2,3},{3,2},{4,5},{5,4},{6,7},{7,6},{8,9},{9,8},{10,11... | collective-permute-start | bytes 1448 | tf_op jit(solution)/shard_map/ppermute | solution.py:774
  322.2 9.5 %copy-start = (f32[480,5120]{1,0:T(8,128)}, f32[480,5120]{1,0:T(8,128)S(1)}, u32[]{:S(2)}) copy-start(f32[480,5120]{1,0:T(8,128)S(1)} %fusion.2) | copy-start | bytes 29491204
  322.2 3.2 copy-start.7
  322.5 28.5 %collective-permute-start.4 = (bf16[240,5120]{1,0:T(8,128)(2,1)S(1)}, bf16[240,5120]{1,0:T(8,128)(2,1)}, u32[]{:S(2)}, u32[]{:S(2)}) collective-permute-start(bf16[240,5120]{1,0:T(8,128)(2,1)S(1)} %dynamic-slice_convert_fusion), channel_id=1, source_target_pairs={{0,1},{1,0},{2,3},{3,2},{4,5},{5,4},{6,7},{7,6},{8,9},{9,8},{10,11... | collective-permute-start | bytes 7372808 | tf_op jit(solution)/shard_map/ppermute | solution.py:774
  331.7 2.3 copy-start.2
  339.1 7.7 %collective-permute-start.5 = (bf16[2560,240]{0,1:T(8,128)(2,1)}, bf16[2560,240]{0,1:T(8,128)(2,1)S(1)}, u32[]{:S(2)}, u32[]{:S(2)}) collective-permute-start(bf16[2560,240]{0,1:T(8,128)(2,1)} %dynamic-slice_convert_fusion.1), channel_id=1, source_target_pairs={{0,1},{1,0},{2,3},{3,2},{4,5},{5,4},{6,7},{7,6},{8,9},{9,8},{10,11... | collective-permute-start | bytes 3686408 | tf_op jit(solution)/shard_map/ppermute | solution.py:774
  344.0 7.1 %copy-start.1 = (f32[480,5120]{1,0:T(8,128)S(1)}, f32[480,5120]{1,0:T(8,128)}, u32[]{:S(2)}) copy-start(f32[480,5120]{1,0:T(8,128)} %copy-done) | copy-start | bytes 29491204

commit v2 on v1

v2 whole, which is shorter than its diff:
```python
import functools

import jax
import jax.numpy as jnp
import numpy as np
from jax import lax
from jax.experimental import pallas as pl
from jax.experimental.pallas import tpu as pltpu
from jax.sharding import PartitionSpec as P

HEADS = 15
KV_HEADS = 5
HEAD_DIM = 64
FF = 2560
D = 960
Q_WIDTH = 960
QKV_WIDTH = 1600
SHORT_LEN = 16
LONG_LEN = 64
EPS = 1e-05
BASE = 10000.0
NEG = -1e30


class Box(dict):
    __getattr__ = dict.__getitem__
    __setattr__ = dict.__setitem__


BF = jnp.bfloat16
F32 = jnp.float32
MICROS = 2
ROWS = MICROS * LONG_LEN
CHUNK = 256
TILE = 128
TILES = 8
K_HALF = 15
V_HALF = 20
MESH = pl.DeviceIdType.MESH
DOWN = "dnT"

KEEP = dict(x=(0, 1024), mid=(1024, 1024), p=(2048, 1024), qkv=(3072, 1664))
KEEP.update(A=(4736, FF), B=(7296, FF))
KEEP_WIDTH = 9856
LEFT = dict(n1=D, mix=D, n2=D, hid=FF)
RIGHT = dict(gqkv=QKV_WIDTH, gat=D, ggu=2 * FF, gff=D)
WEIGHTS = dict(qkv=(D, QKV_WIDTH), out=(Q_WIDTH, D), gu=(D, 2 * FF), dn=(FF, D))


def nn(a, b):
    return lax.dot_general(a, b, (((1,), (0,)), ((), ())), preferred_element_type=F32)


def nt(a, b):
    return lax.dot_general(a, b, (((1,), (1,)), ((), ())), preferred_element_type=F32)


def tn(a, b):
    return lax.dot_general(a, b, (((0,), (0,)), ((), ())), preferred_element_type=F32)


def chunks(total, width=CHUNK):
    return [(c, min(width, total - c)) for c in range(0, total, width)]


def lane(rows):
    return lax.broadcasted_iota(jnp.int32, (rows, TILE), 1)


def inverse_rms(x):
    return lax.rsqrt(jnp.mean(x * x, -1, keepdims=True) + EPS)


def turn(tile):
    first = (lane(tile.shape[0]) % HEAD_DIM) < HEAD_DIM // 2
    return jnp.where(first, pltpu.roll(tile, TILE - 32, 1), pltpu.roll(tile, 32, 1))


def query_scale(column, rows):
    scale = HEAD_DIM**-0.5
    if column + TILE <= Q_WIDTH:
        return scale
    return jnp.where(lane(rows) < HEAD_DIM, scale, 1.0)


def head_pairs(ref, rows, first):
    low = lane(LONG_LEN) < HEAD_DIM
    tiles = {}
    spread = []
    for head in range(KV_HEADS):
        place = first + head
        t = place // 2
        if t not in tiles:
            width = min(TILE, QKV_WIDTH - t * TILE)
            x = ref[rows, t * TILE : t * TILE + width].astype(F32)
            if width < TILE:
                x = jnp.concatenate([x, x], 1)
            tiles[t] = (x, pltpu.roll(x, HEAD_DIM, 1))
        x, swapped = tiles[t]
        spread.append(jnp.where(low, x, swapped) if place % 2 == 0 else jnp.where(low, swapped, x))
    pairs = []
    for t in range(TILES):
        a = 2 * t // 3
        b = min((2 * t + 1) // 3, KV_HEADS - 1)
        pairs.append((spread[a] if a == b else jnp.where(low, spread[a], spread[b])).astype(BF))
    return pairs


def diagonal(ref, rows, t):
    low = lane(LONG_LEN) < HEAD_DIM
    x = ref[rows, t * TILE : (t + 1) * TILE].astype(F32)
    above = jnp.where(low, x, 0.0).astype(BF)
    below = jnp.where(low, 0.0, x).astype(BF)
    if t == TILES - 1:
        below = jnp.zeros_like(below)
    return jnp.concatenate([above, below], 0)


def micro_rows():
    return [slice(b * LONG_LEN, (b + 1) * LONG_LEN) for b in range(MICROS)]


def attention_forward(S):
    low = lane(LONG_LEN) < HEAD_DIM
    for rows in micro_rows():
        keys = head_pairs(S.qkv, rows, K_HALF)
        for t in range(TILES):
            S.e[rows, t * TILE : (t + 1) * TILE] = nt(keys[t], diagonal(S.qkv, rows, t))
    for rows in micro_rows():
        bias = S.bias[rows, :]
        for t in range(TILES):
            s = S.e[rows, t * TILE : (t + 1) * TILE] + bias
            e = jnp.exp(s - jnp.max(s, 0, keepdims=True))
            z = 1.0 / jnp.sum(e, 0, keepdims=True)
            S.p[rows, t * TILE : (t + 1) * TILE] = (e * z).astype(BF)
    for rows in micro_rows():
        values = head_pairs(S.qkv, rows, V_HALF)
        for t in range(TILES):
            o = tn(S.p[rows, t * TILE : (t + 1) * TILE], values[t])
            m = jnp.where(low, o[:LONG_LEN], o[LONG_LEN:]).astype(BF)
            width = min(TILE, Q_WIDTH - t * TILE)
            S.mix[rows, t * TILE : t * TILE + width] = m[:, :width]


def block_forward(W, S, arrived):
    h = S.h
    x = h[...]
    S.x[:, :D] = x.astype(BF)
    S.n1[...] = (x * inverse_rms(x) * W.ga[...]).astype(BF)
    arrived("qkv")
    n1 = S.n1[...]
    for c, w in chunks(QKV_WIDTH):
        o = nn(n1, W.qkv[:, c : c + w])
        for t, tw in chunks(w, TILE):
            column = c + t
            tile = o[:, t : t + tw]
            if column < Q_WIDTH + KV_HEADS * HEAD_DIM:
                tile = tile * S.cos[...] + turn(tile) * S.sin[...]
                if column < Q_WIDTH:
                    tile = tile * query_scale(column, ROWS)
            S.qkv[:, column : column + tw] = tile.astype(BF)
    attention_forward(S)
    arrived("out")
    mix = S.mix[...]
    for c, w in chunks(D):
        h[:, c : c + w] = h[:, c : c + w] + nn(mix, W.out[:, c : c + w])
    x = h[...]
    S.mid[:, :D] = x.astype(BF)
    S.n2[...] = (x * inverse_rms(x) * W.gf[...]).astype(BF)
    arrived("gu")
    n2 = S.n2[...]
    for c, w in chunks(FF):
        gate = nn(n2, W.gu[:, c : c + w])
        up = nn(n2, W.gu[:, FF + c : FF + c + w])
        sg = 1.0 / (1.0 + jnp.exp(-gate))
        act = gate * sg
        S.B[:, c : c + w] = act.astype(BF)
        S.A[:, c : c + w] = (up * sg * (1.0 + gate * (1.0 - sg))).astype(BF)
        S.hid[:, c : c + w] = (act * up).astype(BF)
    arrived("dn")
    hid = S.hid[...]
    for c, w in chunks(D):
        h[:, c : c + w] = h[:, c : c + w] + nn(hid, W.dn[:, c : c + w])


def attention_backward(S):
    low = lane(LONG_LEN) < HEAD_DIM
    for rows in micro_rows():
        values = head_pairs(S.qkv, rows, V_HALF)
        for t in range(TILES):
            S.e[rows, t * TILE : (t + 1) * TILE] = nt(values[t], diagonal(S.gm, rows, t))
    for rows in micro_rows():
        for t in range(TILES):
            gp = S.e[rows, t * TILE : (t + 1) * TILE]
            p = S.p[rows, t * TILE : (t + 1) * TILE].astype(F32)
            total = jnp.sum(gp * p, 0, keepdims=True)
            S.gs[rows, t * TILE : (t + 1) * TILE] = (p * (gp - total)).astype(BF)

    def store(rows, column, value, turned):
        if turned:
            value = value * S.cos[rows, :] - turn(value) * S.sin[rows, :]
        width = min(TILE, QKV_WIDTH - column)
        S.gqkv[rows, column : column + width] = value[:, :width].astype(BF)

    def fold(parts):
        sums = []
        for head in range(KV_HEADS):
            lower, upper = None, None
            for q in (3 * head, 3 * head + 1, 3 * head + 2):
                part = parts[q // 2]
                if q % 2 == 0:
                    lower = part if lower is None else lower + part
                else:
                    upper = part if upper is None else upper + part
            sums.append((jnp.where(low, lower, 0.0), jnp.where(low, 0.0, upper)))
        return sums

    def placed(sums, head, half):
        lower, upper = sums[head]
        if half == 0:
            return lower + pltpu.roll(upper, HEAD_DIM, 1)
        return upper + pltpu.roll(lower, HEAD_DIM, 1)

    for rows in micro_rows():
        keys = head_pairs(S.qkv, rows, K_HALF)
        grad_k, grad_v = [], []
        last = None
        for t in range(TILES):
            gs = S.gs[rows, t * TILE : (t + 1) * TILE]
            grad_k.append(nn(gs, diagonal(S.qkv, rows, t)))
            grad_v.append(
                nn(S.p[rows, t * TILE : (t + 1) * TILE], diagonal(S.gm, rows, t))
            )
            o = tn(gs, keys[t])
            grad_q = jnp.where(low, o[:LONG_LEN], o[LONG_LEN:]) * HEAD_DIM**-0.5
            if t < TILES - 1:
                store(rows, t * TILE, grad_q, True)
            else:
                last = grad_q
        k, v = fold(grad_k), fold(grad_v)
        store(rows, 896, jnp.where(low, last, placed(k, 0, 1)), True)
        store(rows, 1024, placed(k, 1, 0) + placed(k, 2, 1), True)
        store(rows, 1152, placed(k, 3, 0) + placed(k, 4, 1), True)
        store(rows, 1280, placed(v, 0, 0) + placed(v, 1, 1), False)
        store(rows, 1408, placed(v, 2, 0) + placed(v, 3, 1), False)
        store(rows, 1536, placed(v, 4, 0), False)


def rms_backward(x, gain, e, base):
    r = inverse_rms(x)
    scaled = e * gain
    mean = jnp.mean(x * scaled, -1, keepdims=True)
    return base + r * scaled - x * (r * r * r * mean), jnp.sum(e * x * r, 0, keepdims=True)


def block_backward(W, S, gain_attn_grad, gain_ffn_grad):
    g = S.h
    S.gff[...] = g[...].astype(BF)
    gff = S.gff[...]
    for c, w in chunks(FF):
        gh = nn(gff, W.dnT[:, c : c + w])
        S.ggu[:, c : c + w] = (gh * S.A[:, c : c + w].astype(F32)).astype(BF)
        S.ggu[:, FF + c : FF + c + w] = (gh * S.B[:, c : c + w].astype(F32)).astype(BF)
    ggu = S.ggu[...]
    for c, w in chunks(D):
        S.e[:, c : c + w] = nn(ggu, W.guT[:, c : c + w])
    new, gain = rms_backward(S.mid[:, :D].astype(F32), W.gf[...], S.e[:, :D], g[...])
    gain_ffn_grad[...] += gain
    g[...] = new
    S.gat[...] = new.astype(BF)
    gat = S.gat[...]
    for c, w in chunks(Q_WIDTH):
        S.gm[:, c : c + w] = nn(gat, W.outT[:, c : c + w]).astype(BF)
    attention_backward(S)
    gqkv = S.gqkv[...]
    for c, w in chunks(D):
        S.e[:, c : c + w] = nn(gqkv, W.qkvT[:, c : c + w])
    new, gain = rms_backward(S.x[:, :D].astype(F32), W.ga[...], S.e[:, :D], g[...])
    gain_attn_grad[...] += gain
    g[...] = new


def flip(source, target, size=CHUNK):
    depth, width = source.shape
    whole = width // size

    def strip(start, w):
        for k, kw in chunks(depth):
            target[pl.ds(start, w), k : k + kw] = source[k : k + kw, pl.ds(start, w)].T

    def one(i, carry):
        strip(pl.multiple_of(i * size, size), size)
        return carry

    lax.fori_loop(0, whole, one, 0)
    if width % size:
        strip(whole * size, width % size)


def make_constants(S, meta, item, tables):
    cos_long, sin_long, cos_short, sin_short = tables
    shape = (LONG_LEN, TILE)
    slot = lax.broadcasted_iota(jnp.int32, shape, 0)
    other = lane(LONG_LEN) % LONG_LEN
    piece = (slot // SHORT_LEN).astype(F32)
    other_piece = (other // SHORT_LEN).astype(F32)
    for b, rows in enumerate(micro_rows()):
        is_long = jnp.broadcast_to(meta[item, b : b + 1, :], shape) > 0.5
        count = jnp.broadcast_to(meta[item, MICROS + b : MICROS + b + 1, :], shape)
        S.cos[rows, :] = jnp.where(is_long, cos_long[...], cos_short[...])
        S.sin[rows, :] = jnp.where(is_long, sin_long[...], sin_short[...])
        short = jnp.where(other_piece < count, 0.0, jnp.where(slot == other, 0.0, NEG))
        short = jnp.where(piece == other_piece, short, NEG)
        bias = jnp.where(is_long, 0.0, short)
        S.bias[rows, :] = jnp.where(slot <= other, bias, NEG)
        S.valid[rows, :] = jnp.where(is_long, 1.0, jnp.where(piece < count, 1.0, 0.0))


def named(names, refs):
    boxes = []
    for group in names:
        boxes.append(Box(zip(group, refs)))
        refs = refs[len(group) :]
    return boxes


def pipeline_kernel(sections, chips, own, names, *refs):
    I, O, R = named(names, refs)
    far = own * (chips - 1)
    section = lax.axis_index("section")
    data = lax.axis_index("dp")
    chip, core = data // 2, data % 2
    is_first, is_last = section == 0, section == sections - 1
    W = Box({name: R["w_" + name] for name in WEIGHTS})
    W.update({name + "T": R["t_" + name] for name in WEIGHTS})
    W.ga, W.gf = I.ga, I.gf

    def partner(d):
        return lax.rem(chip - d + chips, chips) * 2 + core

    barrier = pltpu.get_barrier_semaphore()

    @pl.when(section > 0)
    def _():
        pl.semaphore_signal(barrier, 1, device_id=dict(section=section - 1), device_id_type=MESH)

    @pl.when(section < sections - 1)
    def _():
        pl.semaphore_signal(barrier, 1, device_id=dict(section=section + 1), device_id_type=MESH)

    for d in range(1, chips):
        pl.semaphore_signal(barrier, 1, device_id=dict(dp=partner(d)), device_id_type=MESH)

    early_names = [name for name in WEIGHTS if name in I]
    weight_names = early_names + [DOWN]
    weight_copies = {
        name: pltpu.make_async_copy(I[name], W[name], R.w_sem.at[k])
        for k, name in enumerate(weight_names)
    }
    slab = W.dn.at[0:D, 0 : own * ROWS]
    token_copy = pltpu.make_async_copy(I.tok, slab, R.t_sem)
    cotangent_copy = pltpu.make_async_copy(I.cot, slab, R.t_sem)

    @pl.when(is_first)
    def _():
        token_copy.start()

    @pl.when(is_last)
    def _():
        cotangent_copy.start()

    for copy in weight_copies.values():
        copy.start()

    def columns_of(ref, j):
        return ref.at[:, pl.ds(pl.multiple_of(j * ROWS, ROWS), ROWS)]

    R.meta[0:own] = I.meta[...]
    O.gga[...] = jnp.zeros_like(O.gga)
    O.ggf[...] = jnp.zeros_like(O.ggf)
    R.gm[...] = jnp.zeros_like(R.gm)

    others = chips - 1
    near = jnp.where(is_first, 0, 1) + jnp.where(is_last, 0, 1)
    pl.semaphore_wait(barrier, near + others)

    def meta_copy(d):
        return pltpu.make_async_remote_copy(
            src_ref=I.meta,
            dst_ref=R.meta.at[pl.ds(own * d, own)],
            send_sem=R.ms_sem.at[d - 1],
            recv_sem=R.m_sem.at[d - 1],
            device_id=dict(dp=partner(d)),
            device_id_type=MESH,
        )

    def next_copy(j):
        return pltpu.make_async_remote_copy(
            src_ref=R.outs.at[j],
            dst_ref=R.fin.at[j],
            send_sem=R.fs_sem.at[j],
            recv_sem=R.f_sem.at[j],
            device_id=dict(section=section + 1),
            device_id_type=MESH,
        )

    def previous_copy(j):
        return pltpu.make_async_remote_copy(
            src_ref=R.outs.at[j],
            dst_ref=R.bin.at[j],
            send_sem=R.bs_sem.at[j],
            recv_sem=R.b_sem.at[j],
            device_id=dict(section=section - 1),
            device_id_type=MESH,
        )

    def far_copy(buffer, recv, send, d, j):
        return pltpu.make_async_remote_copy(
            src_ref=buffer.at[j],
            dst_ref=buffer.at[own * d + j],
            send_sem=send.at[own * (d - 1) + j],
            recv_sem=recv.at[own * d + j],
            device_id=dict(dp=partner(d)),
            device_id_type=MESH,
        )

    def far_forward(d, j):
        return far_copy(R.fin, R.f_sem, R.fx_sem, d, j)

    def far_backward(d, j):
        return far_copy(R.bin, R.b_sem, R.bx_sem, d, j)

    def out_copy(j):
        return pltpu.make_async_copy(R.flip, columns_of(O.out, j), R.o_sem.at[j])

    def grad_copy(j):
        return pltpu.make_async_copy(R.flip, columns_of(O.gin, j), R.g_sem.at[j])

    for d in range(1, chips):
        meta_copy(d).start()

    @pl.when(is_first)
    def _():
        token_copy.wait()
        for j in range(own):
            for c, w in chunks(D):
                R.fin[j, :, c : c + w] = slab[c : c + w, j * ROWS : (j + 1) * ROWS].T

    @pl.when(is_last)
    def _():
        cotangent_copy.wait()
        for j in range(own):
            for c, w in chunks(D):
                R.bin[j, :, c : c + w] = slab[c : c + w, j * ROWS : (j + 1) * ROWS].T

    early = section >= sections // 2

    def views(slot):
        S = Box(R)
        for name, (start, width) in KEEP.items():
            S[name] = R.keep.at[slot, :, start : start + width]
        for name in list(LEFT) + list(RIGHT):
            S[name] = R[name].at[slot]
        return S

    def left_copies(slot, index):
        pairs = [(R.keep.at[slot], O.keep.at[index])]
        pairs += [(R[name].at[slot], O[name].at[index]) for name in LEFT]
        return [
            pltpu.make_async_copy(a, b, R.l_sem.at[slot, k]) for k, (a, b) in enumerate(pairs)
        ]

    def right_copies(slot, index):
        return [
            pltpu.make_async_copy(R[name].at[slot], O[name].at[index], R.r_sem.at[slot, k])
            for k, name in enumerate(RIGHT)
        ]

    def keep_load(slot, index):
        return pltpu.make_async_copy(O.keep.at[index], R.keep.at[slot], R.k_sem.at[slot])

    def turn_out():
        value = R.h[...]

        for c, w in chunks(D):
            R.flip[c : c + w, :] = value[:, c : c + w].astype(BF).T

    def forward_phase(start, count, is_far):
        def step(k, carry):
            item = start + k

            @pl.when(is_far)
            def _():
                d = item // own
                far_forward(d, item - own * d).wait_recv()

            @pl.when(jnp.logical_not(is_far))
            def _():
                @pl.when(jnp.logical_not(is_first))
                def _():
                    next_copy(item).wait_recv()

                for d in range(1, chips):
                    far_forward(d, item).start()

            make_constants(
                R, R.meta, item, (I.cosl, I.sinl, I.coss, I.sins)
            )
            R.h[...] = R.fin[item].astype(F32)

            def one(f, carry):
                @pl.when(k > 0)
                def _():
                    for copy in left_copies(f, 2 * (item - 1) + f):
                        copy.wait()

                fresh = jnp.logical_not(early) & (item == 0) & (f == 0)

                def arrived(name):
                    if name not in early_names:

                        @pl.when(fresh & is_first)
                        def _():
                            weight_copies[DOWN].wait()
                            flip(W.dnT, W.dn)

                    else:

                        @pl.when(fresh)
                        def _():
                            weight_copies[name].wait()

                block_forward(W, views(f), arrived)

                @pl.when(f == 0)
                def _():
                    for copy in left_copies(0, 2 * item):
                        copy.start()

                return carry

            lax.fori_loop(0, 2, one, 0)

            @pl.when(jnp.logical_not(is_far))
            def _():
                R.h[...] = R.h[...] * R.valid[:, 0:1]
                R.outs[item] = R.h[...].astype(BF)

                @pl.when(jnp.logical_not(is_last))
                def _():
                    next_copy(item).start()

                @pl.when(item > 0)
                def _():
                    out_copy(item - 1).wait()

                turn_out()
                out_copy(item).start()

            for copy in left_copies(1, 2 * item + 1):
                copy.start()
            return carry

        lax.fori_loop(0, count, step, 0)
        for f in range(2):
            for copy in left_copies(f, 2 * (start + count - 1) + f):
                copy.wait()

    def backward_phase(start, count, is_far):
        keep_load(1, 2 * start + 1).start()

        def step(k, carry):
            item = start + k

            @pl.when(is_far)
            def _():
                d = item // own
                far_backward(d, item - own * d).wait_recv()

            @pl.when(jnp.logical_not(is_far))
            def _():
                @pl.when(jnp.logical_not(is_last))
                def _():
                    previous_copy(item).wait_recv()

                for d in range(1, chips):
                    far_backward(d, item).start()

            make_constants(
                R, R.meta, item, (I.cosl, I.sinl, I.coss, I.sins)
            )
            R.h[...] = R.bin[item].astype(F32) * R.valid[:, 0:1]

            def one(i, carry):
                f = 1 - i
                keep_load(f, 2 * item + f).wait()

                @pl.when(f == 1)
                def _():
                    keep_load(0, 2 * item).start()

                @pl.when((f == 0) & (k < count - 1))
                def _():
                    keep_load(1, 2 * item + 3).start()

                @pl.when(k > 0)
                def _():
                    for copy in right_copies(f, 2 * (item - 1) + f):
                        copy.wait()

                block_backward(W, views(f), O.gga, O.ggf)

                @pl.when(f == 1)
                def _():
                    for copy in right_copies(1, 2 * item + 1):
                        copy.start()

                return carry

            lax.fori_loop(0, 2, one, 0)

            @pl.when(jnp.logical_not(is_far))
            def _():
                @pl.when(jnp.logical_not(is_last))
                def _():
                    next_copy(item).wait_send()

                R.outs[item] = R.h[...].astype(BF)

                @pl.when(jnp.logical_not(is_first))
                def _():
                    previous_copy(item).start()

                @pl.when(item > 0)
                def _():
                    grad_copy(item - 1).wait()

                @pl.when(item == 0)
                def _():
                    out_copy(own - 1).wait()

                turn_out()
                grad_copy(item).start()

            for copy in right_copies(0, 2 * item):
                copy.start()
            return carry

        lax.fori_loop(0, count, step, 0)
        for f in range(2):
            for copy in right_copies(f, 2 * (start + count - 1) + f):
                copy.wait()

    phases = 4 if far else 2

    def phase(p, carry):
        if far:
            is_far = jnp.where(is_last, p >= 2, lax.rem(p, 2) == 1)
            is_back = jnp.where(is_last, lax.rem(p, 2) == 1, p >= 2)
            start = jnp.where(is_far, own, 0)
            count = jnp.where(is_far, far, own)
        else:
            is_far, is_back, start, count = p < 0, p == 1, 0, own

        @pl.when((p == 0) & jnp.logical_not(is_first))
        def _():
            weight_copies[DOWN].wait()
            flip(W.dnT, W.dn)

        @pl.when((p == 0) & early)
        def _():
            for name in early_names:
                weight_copies[name].wait()

        @pl.when(jnp.where(early, p == 0, p == phases // 2))
        def _():
            for name in early_names:
                flip(W[name], W[name + "T"])

        if far:

            @pl.when(is_far & jnp.logical_not(is_back))
            def _():
                for d in range(1, chips):
                    meta_copy(d).wait_recv()

        @pl.when(jnp.logical_not(is_back))
        def _():
            forward_phase(start, count, is_far)

        @pl.when(is_back)
        def _():
            backward_phase(start, count, is_far)

        return carry

    lax.fori_loop(0, phases, phase, 0)

    for j in range(own):

        @pl.when(jnp.logical_not(is_first))
        def _():
            previous_copy(j).wait_send()

        for d in range(1, chips):
            far_forward(d, j).wait_send()
            far_backward(d, j).wait_send()
    grad_copy(own - 1).wait()
    for d in range(1, chips):
        meta_copy(d).wait_send()


def rotary_tables():
    half = HEAD_DIM // 2
    frequency = BASE ** (-2.0 * np.arange(half, dtype=np.float32) / HEAD_DIM)
    slots = np.arange(LONG_LEN)
    tables = []
    for position in (slots, slots % SHORT_LEN):
        angle = position.astype(np.float32)[:, None] * frequency[None, :].astype(np.float32)
        cos, sin = np.cos(angle), np.sin(angle)
        tables.append(np.tile(np.concatenate([cos, cos], 1), (1, 2)).astype(np.float32))
        tables.append(np.tile(np.concatenate([-sin, sin], 1), (1, 2)).astype(np.float32))
    return tables


def vmem(*shape, dtype=BF):
    return pltpu.VMEM(shape, dtype)


HBM = pl.BlockSpec(memory_space=pl.ANY)
LOCAL = pl.BlockSpec(memory_space=pltpu.VMEM)
VMEM_LIMIT = 127 * 2**19


def run_pipeline(sections, chips, own, hbm_inputs, inputs):
    items = own * chips
    scratch = Box(
        fin=vmem(items, ROWS, D),
        bin=vmem(items, ROWS, D),
        outs=vmem(own, ROWS, D),
        flip=vmem(D, ROWS),
        meta=vmem(items, 8, TILE, dtype=F32),
        keep=vmem(2, ROWS, KEEP_WIDTH),
        h=vmem(ROWS, D, dtype=F32),
        e=vmem(ROWS, 1024, dtype=F32),
        gm=vmem(ROWS, 1024),
        gs=vmem(ROWS, 1024),
        cos=vmem(ROWS, TILE, dtype=F32),
        sin=vmem(ROWS, TILE, dtype=F32),
        bias=vmem(ROWS, TILE, dtype=F32),
        valid=vmem(ROWS, TILE, dtype=F32),
    )
    for name, width in {**LEFT, **RIGHT}.items():
        scratch[name] = vmem(2, ROWS, width)
    for name, (depth, width) in WEIGHTS.items():
        scratch["w_" + name] = vmem(depth, width)
        scratch["t_" + name] = vmem(width, depth)
    far = max(1, own * (chips - 1))
    counts = dict(
        w_sem=(len(WEIGHTS),),
        f_sem=(items,),
        b_sem=(items,),
        fs_sem=(own,),
        bs_sem=(own,),
        fx_sem=(far,),
        bx_sem=(far,),
        m_sem=(max(1, chips - 1),),
        ms_sem=(max(1, chips - 1),),
        o_sem=(own,),
        g_sem=(own,),
        l_sem=(2, 1 + len(LEFT)),
        r_sem=(2, len(RIGHT)),
        k_sem=(2,),
    )
    for name, shape in counts.items():
        scratch[name] = pltpu.SemaphoreType.DMA(shape)
    scratch.t_sem = pltpu.SemaphoreType.DMA
    shapes = Box(out=(D, own * ROWS), gin=(D, own * ROWS))
    for name, width in {**LEFT, **RIGHT}.items():
        shapes[name] = (2 * items, ROWS, width)
    shapes.keep = (2 * items, ROWS, KEEP_WIDTH)
    out_shape = Box({name: jax.ShapeDtypeStruct(shape, BF) for name, shape in shapes.items()})
    out_shape.gga = out_shape.ggf = jax.ShapeDtypeStruct((1, D), F32)
    names = [[*hbm_inputs, *inputs], list(out_shape), list(scratch)]
    results = pl.pallas_call(
        functools.partial(pipeline_kernel, sections, chips, own, names),
        out_shape=list(out_shape.values()),
        in_specs=[HBM] * len(hbm_inputs) + [LOCAL] * len(inputs),
        out_specs=[HBM] * len(shapes) + [LOCAL] * 2,
        scratch_shapes=list(scratch.values()),
        compiler_params=pltpu.CompilerParams(
            collective_id=0, has_side_effects=True, vmem_limit_bytes=VMEM_LIMIT
        ),
    )(*hbm_inputs.values(), *inputs.values())
    return Box(zip(out_shape, results))


PRODUCTS = dict(out=(*"gat mix".split(), Q_WIDTH), qkv=(*"n1 gqkv".split(), QKV_WIDTH))
PRODUCTS.update(dn=(*"gff hid".split(), FF), gu=(*"n2 ggu".split(), 2 * FF))
SPAN = 10


def spans_of(base, width):
    return [(base + i, n) for i, n in chunks(len(chunks(width)), SPAN)]


def gradient_kernel(depth, share, names, *refs):
    I, O, R = named(names, refs)
    data = lax.axis_index("dp")
    chip, core = data // 2, data % 2
    sibling = dict(dp=chip * 2 + 1 - core)
    barrier = pltpu.get_barrier_semaphore()
    pl.semaphore_signal(barrier, 1, device_id=sibling, device_id_type=MESH)
    order = [n for pair in PRODUCTS.values() for n in pair[:2]]
    loads = {
        name: pltpu.make_async_copy(I[name], R[name], R.load.at[k]) for k, name in enumerate(order)
    }
    for name in order[:4]:
        loads[name].start()
    later = order[4:]
    R.gain[0:1] = I.gga[...]
    R.gain[1:2] = I.ggf[...]
    pl.semaphore_wait(barrier, 1)

    def to_sibling(source, target, send, recv):
        return pltpu.make_async_remote_copy(
            src_ref=source,
            dst_ref=target,
            send_sem=send,
            recv_sem=recv,
            device_id=sibling,
            device_id_type=MESH,
        )

    gain_copy = to_sibling(R.gain, R.got_gain, R.gs, R.gr)
    gain_copy.start()

    def span_copy(first, n):
        blocks = pl.ds(first, n)
        return to_sibling(R.sent.at[blocks], R.got.at[blocks], R.ss.at[first], R.rs.at[first])

    mine = pl.ds(pl.multiple_of((2 * chip + core) * share, 16), share)
    other = pl.ds(pl.multiple_of((2 * chip + 1 - core) * share, 16), share)
    base = 0
    bases = {}
    for name, (left, right, width) in PRODUCTS.items():
        turned = R["t_" + left]
        loads[left].wait()
        for r, rw in chunks(depth):
            for c, w in chunks(D):
                turned[c : c + w, r : r + rw] = R[left][r : r + rw, c : c + w].T
        loads[right].wait()
        for more in later[:2]:
            loads[more].start()
        later = later[2:]
        for first, n in spans_of(base, width):
            for i in range(first, first + n):
                c = (i - base) * CHUNK
                w = min(CHUNK, width - c)
                R.sent[i, :, 0:w] = nn(turned[other, :], R[right][:, c : c + w]).astype(BF)
            span_copy(first, n).start()
        bases[name] = base
        base += len(chunks(width))
    for name, (left, right, width) in PRODUCTS.items():
        base = bases[name]
        for first, n in spans_of(base, width):
            span_copy(first, n).wait_recv()
            for i in range(first, first + n):
                c = (i - base) * CHUNK
                w = min(CHUNK, width - c)
                total = nn(R["t_" + left][mine, :], R[right][:, c : c + w])
                O[name][:, c : c + w] = (total + R.got[i, :, 0:w].astype(F32)).astype(BF)
    gain_copy.wait()
    O.gain[...] = R.gain[...] + R.got_gain[...]
    for name, (_, _, width) in PRODUCTS.items():
        for first, n in spans_of(bases[name], width):
            span_copy(first, n).wait_send()


def run_gradients(share, operands, gga, ggf):
    depth = operands.n1.shape[0]
    order = [n for pair in PRODUCTS.values() for n in pair[:2]]
    blocks = sum(len(chunks(width)) for _, _, width in PRODUCTS.values())
    scratch = Box({n: vmem(*operands[n].shape) for n in order})
    for left, _, _ in PRODUCTS.values():
        scratch["t_" + left] = vmem(D, depth)
    scratch.update(
        sent=vmem(blocks, share, CHUNK),
        got=vmem(blocks, share, CHUNK),
        gain=vmem(2, D, dtype=F32),
        got_gain=vmem(2, D, dtype=F32),
        load=pltpu.SemaphoreType.DMA((len(order),)),
        ss=pltpu.SemaphoreType.DMA((blocks,)),
        rs=pltpu.SemaphoreType.DMA((blocks,)),
        gs=pltpu.SemaphoreType.DMA,
        gr=pltpu.SemaphoreType.DMA,
    )
    inputs = Box({n: operands[n] for n in order})
    inputs.update(gga=gga, ggf=ggf)
    shapes = {n: jax.ShapeDtypeStruct((share, w), BF) for n, (_, _, w) in PRODUCTS.items()}
    shapes.update(gain=jax.ShapeDtypeStruct((2, D), F32))
    names = [list(inputs), list(shapes), list(scratch)]
    results = pl.pallas_call(
        functools.partial(gradient_kernel, depth, share, names),
        out_shape=list(shapes.values()),
        in_specs=[HBM] * len(order) + [LOCAL] * 2,
        out_specs=[LOCAL] * len(shapes),
        scratch_shapes=list(scratch.values()),
        compiler_params=pltpu.CompilerParams(
            collective_id=1, has_side_effects=True, vmem_limit_bytes=VMEM_LIMIT
        ),
    )(*inputs.values())
    return Box(zip(shapes, results))


def finish_kernel(groups, share, names, *refs):
    I, O, R = named(names, refs)
    data = lax.axis_index("dp")
    passing = [name for name in I if name not in PRODUCTS and name in O]
    passed_in = [
        pltpu.make_async_copy(I[name], R["i_" + name], R.pass_sem.at[2 * k])
        for k, name in enumerate(passing)
    ]
    passed_out = [
        pltpu.make_async_copy(R["i_" + name], O[name], R.pass_sem.at[2 * k + 1])
        for k, name in enumerate(passing)
    ]
    loads, stores = [], []
    for name, (_, _, width) in PRODUCTS.items():
        for c, w in chunks(width, FF):
            k = len(loads)
            source, target = I[name].at[:, c : c + w], O[name].at[:, c : c + w]
            place = R["o_" + name].at[:, c : c + w]
            if name == TURNED:
                target, place = O[name], R["o_" + name]
            loads.append(
                (name, c, w, pltpu.make_async_copy(source, R["i_" + name].at[:, c : c + w], R.load.at[k]))
            )
            stores.append(pltpu.make_async_copy(place, target, R.store.at[k]))
    for load in loads:
        load[3].start()
    for copy in passed_in:
        copy.start()
    for (name, c, w, load), store in zip(loads, stores):
        load.wait()
        for b, bw in chunks(w, 2 * CHUNK):
            columns = slice(c + b, c + b + bw)
            value = R["i_" + name][:, columns].astype(F32)
            if name == TURNED:
                R["o_" + name][columns, :] = value.T
            else:
                R["o_" + name][:, columns] = value
        store.start()
    for row, gain in enumerate((O.ga, O.gf)):
        value = I.gain[row : row + 1, 0:share]
        for q in range(1, groups):
            value = jnp.where(data == q, I.gain[row : row + 1, q * share : (q + 1) * share], value)
        gain[...] = value
    for arrival, copy in zip(passed_in, passed_out):
        arrival.wait()
        copy.start()
    for copy in stores + passed_out:
        copy.wait()


TURNED = "out"


def run_finish(groups, share, sums, rows):
    inputs = Box({n: sums[n] for n in PRODUCTS})
    inputs.update(rows, gain=sums.gain)
    shapes = Box()
    scratch = Box()
    for name, (_, _, width) in PRODUCTS.items():
        shape = (width, share) if name == TURNED else (share, width)
        shapes[name] = jax.ShapeDtypeStruct(shape, F32)
        scratch["i_" + name] = vmem(share, width)
        scratch["o_" + name] = vmem(*shape, dtype=F32)
    for name, value in rows.items():
        shapes[name] = jax.ShapeDtypeStruct(value.shape, BF)
        scratch["i_" + name] = vmem(*value.shape)
    shapes.ga = shapes.gf = jax.ShapeDtypeStruct((1, share), F32)
    copies = sum(len(chunks(width, FF)) for _, _, width in PRODUCTS.values())
    scratch.update(
        load=pltpu.SemaphoreType.DMA((copies,)),
        store=pltpu.SemaphoreType.DMA((copies,)),
        pass_sem=pltpu.SemaphoreType.DMA((2 * len(rows),)),
    )
    names = [list(inputs), list(shapes), list(scratch)]
    results = pl.pallas_call(
        functools.partial(finish_kernel, groups, share, names),
        out_shape=list(shapes.values()),
        in_specs=[HBM] * (len(inputs) - 1) + [LOCAL],
        out_specs=[HBM] * (len(shapes) - 2) + [LOCAL] * 2,
        scratch_shapes=list(scratch.values()),
        compiler_params=pltpu.CompilerParams(vmem_limit_bytes=VMEM_LIMIT),
    )(*inputs.values())
    return Box(zip(shapes, results))


def gradients_by_xla(groups, share, operands, rows, gga, ggf):
    data = lax.axis_index("dp")
    begin = (data // 2) * 2 * share
    swap = [(i, i ^ 1) for i in range(groups)]

    def exchange(both, axis=0):
        mine = lax.dynamic_slice_in_dim(both, (data % 2) * share, share, axis)
        other = lax.dynamic_slice_in_dim(both, (1 - data % 2) * share, share, axis)
        return mine + lax.ppermute(other.astype(BF), "dp", swap).astype(F32)

    sums = Box(rows)
    for name, (left, right, _) in PRODUCTS.items():
        part = lax.dynamic_slice_in_dim(operands[left], begin, 2 * share, 1)
        sums[name] = exchange(tn(part, operands[right]))
    sums[TURNED] = sums[TURNED].T
    sums.ga = exchange(lax.dynamic_slice_in_dim(gga, begin, 2 * share, 1), 1)
    sums.gf = exchange(lax.dynamic_slice_in_dim(ggf, begin, 2 * share, 1), 1)
    return sums


def body(tokens, cotangent, seq_counts, attn_gain, w_qkv, w_out, ffn_gain, w_gate_up, w_down):
    sections = lax.axis_size("section")
    groups = lax.axis_size("dp")
    chips = groups // 2
    own = tokens.shape[0] // ROWS
    meta = seq_counts.astype(F32).reshape(own, MICROS, 2).transpose(0, 2, 1)
    meta = jnp.pad(meta.reshape(own, 2 * MICROS), ((0, 0), (0, 8 - 2 * MICROS)))
    meta = jnp.broadcast_to(meta[:, :, None], (own, 8, TILE))
    cosl, sinl, coss, sins = rotary_tables()
    hbm_inputs = Box(tok=tokens.T, cot=cotangent.T, dnT=w_down[0].T)
    hbm_inputs.update(qkv=w_qkv[0], out=w_out[0], gu=w_gate_up[0])
    inputs = Box(meta=meta, ga=attn_gain, gf=ffn_gain)
    inputs.update(cosl=cosl, sinl=sinl, coss=coss, sins=sins)
    O = run_pipeline(sections, chips, own, hbm_inputs, inputs)
    share = D // groups
    operands = Box({n: O[n].reshape(-1, O[n].shape[-1]) for n in (*LEFT, *RIGHT)})
    rows = Box(rows_out=O.out, rows_gin=O.gin)
    if share % 16:
        sums = gradients_by_xla(groups, share, operands, rows, O.gga, O.ggf)
    else:
        sums = run_finish(groups, share, run_gradients(share, operands, O.gga, O.ggf), rows)
    return (
        sums.rows_out.T[None],
        sums.rows_gin.T[None],
        sums.ga,
        sums.qkv[None],
        sums.out[None],
        sums.gf,
        sums.gu[None],
        sums.dn.T[None],
    )


def solution(mesh):
    in_specs = (
        P("dp", None),
        P("dp", None),
        P("dp", None),
        P("section", None),
        P("section", None, None),
        P("section", None, None),
        P("section", None),
        P("section", None, None),
        P("section", None, None),
    )
    out_specs = (
        P("section", "dp", None),
        P("section", "dp", None),
        P("section", "dp"),
        P("section", "dp", None),
        P("section", None, "dp"),
        P("section", "dp"),
        P("section", "dp", None),
        P("section", None, "dp"),
    )
    return jax.shard_map(body, mesh=mesh, in_specs=in_specs, out_specs=out_specs, check_vma=False)
```

time: 356 us -> 325 us (0.913)
  Pallas kernels: 291 us -> 322 us
  local copies, waits for them, and re-layouts: 26.2 us -> 0.85 us
  matrix products: 19.3 us -> 0 us
  other arithmetic: 17 us -> 0.68 us
    pallas_call x1 -> x3, Pallas kernels: 291 us -> 322 us  [the longest x1 293 us: run_pipeline(): pl.pallas_call(functools.partial(pipeline_kernel, sections, chips, own, n...]
    unnamed x29 -> x0, local copies, waits for them, and re-layouts: 20.8 us -> none
    dot_general x4 -> x0, matrix products: 19.3 us -> none  [tn(): lax.dot_general(a, b, (((0,), (0,)), ((), ())), preferred_element_type=F32)]
    broadcast_in_dim x4 -> x0, other arithmetic: 14.5 us -> none  [the longest x1 4.6 us: body(): gate_up_grad[None]]
    convert_element_type x6 -> x0, local copies, waits for them, and re-layouts: 4.55 us -> none  [exchange(): return mine + lax.ppermute(other.astype(BF), 'dp', flip).astype(F32)]
  transfers between devices with their start and end apart: 6 -> 0, of which waited for: 0 -> 0; matrix products, arithmetic and copies ran while one was open for 11% -> 0% of each run, Pallas kernels for 0% -> 0%
where the time goes in v2:
time: 325 us
  Pallas kernels  322 us (99%)
    pallas_call x1, Pallas kernels, run_pipeline(): pl.pallas_call(functools.partial(pipeline_kernel, sections, chips, own, n...  293 us
    pallas_call x1, Pallas kernels, run_gradients(): pl.pallas_call(functools.partial(gradient_kernel, depth, share, names), o...  22.4 us
    pallas_call x1, Pallas kernels, run_finish(): pl.pallas_call(functools.partial(finish_kernel, groups, share, names), ou...  6.84 us

profile of v2, /device:TPU:0, one launch (start us, length us, event | category | flops | bytes accessed | tf_op | source)
XLA Modules:
  0.0 324.8 jit_solution(4764206630364612770)
XLA Ops:
  0.6 0.7 convert_element_type.5
  1.3 0.1 reshape.47
  1.4 0.1 reshape.48
  1.5 0.7 broadcast_in_dim.24.refs_6_
  2.2 293.2 %shard_map.188 = (bf16[960,256]{1,0:T(8,128)(2,1)}, bf16[960,256]{1,0:T(8,128)(2,1)}, bf16[8,128,960]{2,1,0:T(8,128)(2,1)}, bf16[8,128,960]{2,1,0:T(8,128)(2,1)}...) custom-call(bf16[960,256]{1,0:T(8,128)(2,1)} %bitcast.43, ...), custom_call_target="tpu_custom_call" | custom-call | tf_op jit(solution)/shard_map/pallas_call | solution.py:785
  295.4 22.4 %shard_map.189 = (bf16[240,960]{1,0:T(8,128)(2,1)}, bf16[240,1600]{1,0:T(8,128)(2,1)}, bf16[240,2560]{1,0:T(8,128)(2,1)}, bf16[240,5120]{1,0:T(8,128)(2,1)}, f32[2,960]{1,0:T(2,128)}) custom-call(bf16[1024,960]{1,0:T(8,128)(2,1)} %bitcast.40, bf16[1024,960]{1,0:T(8,128)(2,1)} %bitcast.38, bf16[1024,960]{1,0:T(8,128)(2,1)} %bitcast.37, ...), custom_call_target="tpu_custom_call" | custom-call | tf_op jit(solution)/shard_map/pallas_call | solution.py:903
  317.8 6.8 %shard_map.190 = (f32[960,240]{1,0:T(8,128)}, f32[240,1600]{1,0:T(8,128)}, f32[240,2560]{1,0:T(8,128)}, f32[240,5120]{1,0:T(8,128)}, bf16[960,256]{1,0:T(8,128)(...) custom-call(bf16[240,960]{1,0:T(8,128)(2,1)} %get-tuple-element.43.refs_0_, ...), custom_call_target="tpu_custom_call" | custom-call | tf_op jit(solution)/shard_map/pallas_call | solution.py:990
  (2 shorter events, 0.0 us)

commit v3 on v2

--- a/solution.py
+++ b/solution.py
@@ -38,6 +38,7 @@
 V_HALF = 20
 MESH = pl.DeviceIdType.MESH
 DOWN = "dnT"
+HELD = 6
 
 KEEP = dict(x=(0, 1024), mid=(1024, 1024), p=(2048, 1024), qkv=(3072, 1664))
 KEEP.update(A=(4736, FF), B=(7296, FF))
@@ -280,8 +281,9 @@
     g[...] = new
 
 
-def flip(source, target, size=CHUNK):
+def flip(source, target, first=0, end=None):
     depth, width = source.shape
+    size = CHUNK
     whole = width // size
 
     def strip(start, w):
@@ -292,7 +294,7 @@
         strip(pl.multiple_of(i * size, size), size)
         return carry
 
-    lax.fori_loop(0, whole, one, 0)
+    lax.fori_loop(first, whole if end is None else end, one, 0)
     if width % size:
         strip(whole * size, width % size)
 
@@ -335,21 +337,30 @@
     W.update({name + "T": R["t_" + name] for name in WEIGHTS})
     W.ga, W.gf = I.ga, I.gf
 
+    crossed = lax.rem(section, 2) == 1
+    sibling = chip * 2 + 1 - core
+    holder = jnp.where(crossed, 1 - core, core)
+    before, after = dict(section=section - 1, dp=sibling), dict(section=section + 1, dp=sibling)
+
+    def far_chip(d):
+        return lax.rem(chip - d + chips, chips) * 2
+
     def partner(d):
-        return lax.rem(chip - d + chips, chips) * 2 + core
+        return far_chip(d) + core
 
     barrier = pltpu.get_barrier_semaphore()
 
     @pl.when(section > 0)
     def _():
-        pl.semaphore_signal(barrier, 1, device_id=dict(section=section - 1), device_id_type=MESH)
+        pl.semaphore_signal(barrier, 1, device_id=before, device_id_type=MESH)
 
     @pl.when(section < sections - 1)
     def _():
-        pl.semaphore_signal(barrier, 1, device_id=dict(section=section + 1), device_id_type=MESH)
-
-    for d in range(1, chips):
-        pl.semaphore_signal(barrier, 1, device_id=dict(dp=partner(d)), device_id_type=MESH)
+        pl.semaphore_signal(barrier, 1, device_id=after, device_id_type=MESH)
+
+    for d in range(1, 2 * chips):
+        other = lax.rem(data + d, 2 * chips)
+        pl.semaphore_signal(barrier, 1, device_id=dict(dp=other), device_id_type=MESH)
 
     early_names = [name for name in WEIGHTS if name in I]
     weight_names = early_names + [DOWN]
@@ -369,28 +380,29 @@
     def _():
         cotangent_copy.start()
 
-    for copy in weight_copies.values():
-        copy.start()
+    for name in early_names[:2]:
+        weight_copies[name].start()
 
     def columns_of(ref, j):
         return ref.at[:, pl.ds(pl.multiple_of(j * ROWS, ROWS), ROWS)]
 
-    R.meta[0:own] = I.meta[...]
     O.gga[...] = jnp.zeros_like(O.gga)
     O.ggf[...] = jnp.zeros_like(O.ggf)
     R.gm[...] = jnp.zeros_like(R.gm)
 
-    others = chips - 1
+    others = 2 * chips - 1
     near = jnp.where(is_first, 0, 1) + jnp.where(is_last, 0, 1)
     pl.semaphore_wait(barrier, near + others)
+    for name in weight_names[2:]:
+        weight_copies[name].start()
 
     def meta_copy(d):
         return pltpu.make_async_remote_copy(
             src_ref=I.meta,
             dst_ref=R.meta.at[pl.ds(own * d, own)],
-            send_sem=R.ms_sem.at[d - 1],
-            recv_sem=R.m_sem.at[d - 1],
-            device_id=dict(dp=partner(d)),
+            send_sem=R.ms_sem.at[d],
+            recv_sem=R.m_sem.at[d],
+            device_id=dict(dp=far_chip(d) + holder),
             device_id_type=MESH,
         )
 
@@ -400,7 +412,7 @@
             dst_ref=R.fin.at[j],
             send_sem=R.fs_sem.at[j],
             recv_sem=R.f_sem.at[j],
-            device_id=dict(section=section + 1),
+            device_id=after,
             device_id_type=MESH,
         )
 
@@ -410,7 +422,7 @@
             dst_ref=R.bin.at[j],
             send_sem=R.bs_sem.at[j],
             recv_sem=R.b_sem.at[j],
-            device_id=dict(section=section - 1),
+            device_id=before,
             device_id_type=MESH,
         )
 
@@ -430,14 +442,43 @@
     def far_backward(d, j):
         return far_copy(R.bin, R.b_sem, R.bx_sem, d, j)
 
+    class RowCopy:
+        def __init__(self, target, j, sent, arrived):
+            place = columns_of(target, j)
+            self.here = pltpu.make_async_copy(R.flip, place, sent.at[j])
+            self.there = pltpu.make_async_remote_copy(
+                src_ref=R.flip,
+                dst_ref=place,
+                send_sem=sent.at[j],
+                recv_sem=arrived.at[j],
+                device_id=dict(dp=sibling),
+                device_id_type=MESH,
+            )
+
+        def start(self):
+            pl.when(crossed)(self.there.start)
+            pl.when(jnp.logical_not(crossed))(self.here.start)
+
+        def wait(self):
+            pl.when(crossed)(self.there.wait_send)
+            pl.when(jnp.logical_not(crossed))(self.here.wait)
+
     def out_copy(j):
-        return pltpu.make_async_copy(R.flip, columns_of(O.out, j), R.o_sem.at[j])
+        return RowCopy(O.out, j, R.o_sem, R.oa_sem)
 
     def grad_copy(j):
-        return pltpu.make_async_copy(R.flip, columns_of(O.gin, j), R.g_sem.at[j])
+        return RowCopy(O.gin, j, R.g_sem, R.ga_sem)
 
     for d in range(1, chips):
         meta_copy(d).start()
+
+    @pl.when(crossed)
+    def _():
+        meta_copy(0).start()
+
+    @pl.when(jnp.logical_not(crossed))
+    def _():
+        R.meta[0:own] = I.meta[...]
 
     @pl.when(is_first)
     def _():
@@ -446,13 +487,34 @@
             for c, w in chunks(D):
                 R.fin[j, :, c : c + w] = slab[c : c + w, j * ROWS : (j + 1) * ROWS].T
 
+    def cotangent_cross(j):
+        return pltpu.make_async_remote_copy(
+            src_ref=R.outs.at[j],
+            dst_ref=R.bin.at[j],
+            send_sem=R.fs_sem.at[j],
+            recv_sem=R.b_sem.at[j],
+            device_id=dict(dp=sibling),
+            device_id_type=MESH,
+        )
+
     @pl.when(is_last)
     def _():
         cotangent_copy.wait()
+        target = R.outs if sections % 2 == 0 else R.bin
         for j in range(own):
             for c, w in chunks(D):
-                R.bin[j, :, c : c + w] = slab[c : c + w, j * ROWS : (j + 1) * ROWS].T
-
+                target[j, :, c : c + w] = slab[c : c + w, j * ROWS : (j + 1) * ROWS].T
+        if sections % 2 == 0:
+            for j in range(own):
+                cotangent_cross(j).start()
+            for j in range(own):
+                cotangent_cross(j).wait()
+
+    @pl.when(crossed)
+    def _():
+        meta_copy(0).wait()
+
+    held = is_first & (core == 1)
     early = section >= sections // 2
 
     def views(slot):
@@ -488,6 +550,7 @@
     def forward_phase(start, count, is_far):
         def step(k, carry):
             item = start + k
+            make_constants(R, R.meta, item, (I.cosl, I.sinl, I.coss, I.sins))
 
             @pl.when(is_far)
             def _():
@@ -503,9 +566,6 @@
                 for d in range(1, chips):
                     far_forward(d, item).start()
 
-            make_constants(
-                R, R.meta, item, (I.cosl, I.sinl, I.coss, I.sins)
-            )
             R.h[...] = R.fin[item].astype(F32)
 
             def one(f, carry):
@@ -526,7 +586,9 @@
 
                     else:
 
-                        @pl.when(fresh)
+                        waits = fresh & jnp.logical_not(held) if name == early_names[-1] else fresh
+
+                        @pl.when(waits)
                         def _():
                             weight_copies[name].wait()
 
@@ -571,6 +633,7 @@
 
         def step(k, carry):
             item = start + k
+            make_constants(R, R.meta, item, (I.cosl, I.sinl, I.coss, I.sins))
 
             @pl.when(is_far)
             def _():
@@ -586,9 +649,6 @@
                 for d in range(1, chips):
                     far_backward(d, item).start()
 
-            make_constants(
-                R, R.meta, item, (I.cosl, I.sinl, I.coss, I.sins)
-            )
             R.h[...] = R.bin[item].astype(F32) * R.valid[:, 0:1]
 
             def one(i, carry):
@@ -672,10 +732,19 @@
             for name in early_names:
                 weight_copies[name].wait()
 
+        largest = early_names[-1]
+
+        @pl.when((p == 0) & held)
+        def _():
+            weight_copies[largest].wait()
+            flip(W[largest], W[largest + "T"], 0, HELD)
+
         @pl.when(jnp.where(early, p == 0, p == phases // 2))
         def _():
-            for name in early_names:
+            for name in early_names[:-1]:
                 flip(W[name], W[name + "T"])
+
+            flip(W[largest], W[largest + "T"], jnp.where(held, HELD, 0))
 
         if far:
 
@@ -708,6 +777,12 @@
     grad_copy(own - 1).wait()
     for d in range(1, chips):
         meta_copy(d).wait_send()
+
+    @pl.when(crossed)
+    def _():
+        for j in range(own):
+            out_copy(j).there.wait_recv()
+            grad_copy(j).there.wait_recv()
 
 
 def rotary_tables():
@@ -764,10 +839,12 @@
         bs_sem=(own,),
         fx_sem=(far,),
         bx_sem=(far,),
-        m_sem=(max(1, chips - 1),),
-        ms_sem=(max(1, chips - 1),),
+        m_sem=(chips,),
+        ms_sem=(chips,),
         o_sem=(own,),
         g_sem=(own,),
+        oa_sem=(own,),
+        ga_sem=(own,),
         l_sem=(2, 1 + len(LEFT)),
         r_sem=(2, len(RIGHT)),
         k_sem=(2,),

time: 325 us -> 311 us (0.957)
  Pallas kernels: 322 us -> 307 us
    pallas_call x1, Pallas kernels: 293 us -> 275 us  [run_pipeline(): pl.pallas_call(functools.partial(pipeline_kernel, sections, chips, own, n...]
where the time goes in v3:
time: 311 us; the launch traced here: 309 us
  Pallas kernels  307 us (99%)
    pallas_call x1, Pallas kernels, run_pipeline(): pl.pallas_call(functools.partial(pipeline_kernel, sections, chips, own, n...  275 us
    pallas_call x1, Pallas kernels, run_gradients(): pl.pallas_call(functools.partial(gradient_kernel, depth, share, names), o...  25.3 us
    pallas_call x1, Pallas kernels, run_finish(): pl.pallas_call(functools.partial(finish_kernel, groups, share, names), ou...  6.84 us

profile of v3, /device:TPU:0, one launch (start us, length us, event | category | flops | bytes accessed | tf_op | source)
XLA Modules:
  0.0 309.5 jit_solution(17790482691463564529)
XLA Ops:
  0.6 0.7 convert_element_type.5
  1.3 0.1 reshape.47
  1.4 0.1 reshape.48
  1.5 0.7 broadcast_in_dim.24.refs_6_
  2.2 275.0 %shard_map.188 = (bf16[960,256]{1,0:T(8,128)(2,1)}, bf16[960,256]{1,0:T(8,128)(2,1)}, bf16[8,128,960]{2,1,0:T(8,128)(2,1)}, bf16[8,128,960]{2,1,0:T(8,128)(2,1)}...) custom-call(bf16[960,256]{1,0:T(8,128)(2,1)} %bitcast.43, ...), custom_call_target="tpu_custom_call" | custom-call | tf_op jit(solution)/shard_map/pallas_call | solution.py:862
  277.2 25.3 %shard_map.189 = (bf16[240,960]{1,0:T(8,128)(2,1)}, bf16[240,1600]{1,0:T(8,128)(2,1)}, bf16[240,2560]{1,0:T(8,128)(2,1)}, bf16[240,5120]{1,0:T(8,128)(2,1)}, f32[2,960]{1,0:T(2,128)}) custom-call(bf16[1024,960]{1,0:T(8,128)(2,1)} %bitcast.40, bf16[1024,960]{1,0:T(8,128)(2,1)} %bitcast.38, bf16[1024,960]{1,0:T(8,128)(2,1)} %bitcast.37, ...), custom_call_target="tpu_custom_call" | custom-call | tf_op jit(solution)/shard_map/pallas_call | solution.py:980
  302.4 6.8 %shard_map.190 = (f32[960,240]{1,0:T(8,128)}, f32[240,1600]{1,0:T(8,128)}, f32[240,2560]{1,0:T(8,128)}, f32[240,5120]{1,0:T(8,128)}, bf16[960,256]{1,0:T(8,128)(...) custom-call(bf16[240,960]{1,0:T(8,128)(2,1)} %get-tuple-element.43.refs_0_, ...), custom_call_target="tpu_custom_call" | custom-call | tf_op jit(solution)/shard_map/pallas_call | solution.py:1067
  (2 shorter events, 0.0 us)

commit v4 on v3

--- a/solution.py
+++ b/solution.py
@@ -38,11 +38,9 @@
 V_HALF = 20
 MESH = pl.DeviceIdType.MESH
 DOWN = "dnT"
-HELD = 6
-
-KEEP = dict(x=(0, 1024), mid=(1024, 1024), p=(2048, 1024), qkv=(3072, 1664))
-KEEP.update(A=(4736, FF), B=(7296, FF))
-KEEP_WIDTH = 9856
+HELD = 12
+
+KEEP = dict(x=D, mid=D, p=1024, qkv=1664, A=FF, B=FF)
 LEFT = dict(n1=D, mix=D, n2=D, hid=FF)
 RIGHT = dict(gqkv=QKV_WIDTH, gat=D, ggu=2 * FF, gff=D)
 WEIGHTS = dict(qkv=(D, QKV_WIDTH), out=(Q_WIDTH, D), gu=(D, 2 * FF), dn=(FF, D))
@@ -392,13 +390,28 @@
 
     others = 2 * chips - 1
     near = jnp.where(is_first, 0, 1) + jnp.where(is_last, 0, 1)
-    pl.semaphore_wait(barrier, near + others)
+
+    @pl.when(is_first)
+    def _():
+        token_copy.wait()
+        for j in range(own):
+            for c, w in chunks(D):
+                R.fin[j, :, c : c + w] = slab[c : c + w, j * ROWS : (j + 1) * ROWS].T
+
     for name in weight_names[2:]:
         weight_copies[name].start()
+    pl.semaphore_wait(barrier, near + others)
+
+    for j in range(own):
+        for b in range(MICROS):
+            for column in range(2):
+                count = I.counts[column : column + 1, MICROS * j + b : MICROS * j + b + 1]
+                row = column * MICROS + b
+                R.mine[j, row : row + 1, :] = jnp.broadcast_to(count.astype(F32), (1, TILE))
 
     def meta_copy(d):
         return pltpu.make_async_remote_copy(
-            src_ref=I.meta,
+            src_ref=R.mine,
             dst_ref=R.meta.at[pl.ds(own * d, own)],
             send_sem=R.ms_sem.at[d],
             recv_sem=R.m_sem.at[d],
@@ -478,14 +491,7 @@
 
     @pl.when(jnp.logical_not(crossed))
     def _():
-        R.meta[0:own] = I.meta[...]
-
-    @pl.when(is_first)
-    def _():
-        token_copy.wait()
-        for j in range(own):
-            for c, w in chunks(D):
-                R.fin[j, :, c : c + w] = slab[c : c + w, j * ROWS : (j + 1) * ROWS].T
+        R.meta[0:own] = R.mine[...]
 
     def cotangent_cross(j):
         return pltpu.make_async_remote_copy(
@@ -519,17 +525,14 @@
 
     def views(slot):
         S = Box(R)
-        for name, (start, width) in KEEP.items():
-            S[name] = R.keep.at[slot, :, start : start + width]
-        for name in list(LEFT) + list(RIGHT):
+        for name in (*KEEP, *LEFT, *RIGHT):
             S[name] = R[name].at[slot]
         return S
 
     def left_copies(slot, index):
-        pairs = [(R.keep.at[slot], O.keep.at[index])]
-        pairs += [(R[name].at[slot], O[name].at[index]) for name in LEFT]
         return [
-            pltpu.make_async_copy(a, b, R.l_sem.at[slot, k]) for k, (a, b) in enumerate(pairs)
+            pltpu.make_async_copy(R[name].at[slot], O[name].at[index], R.l_sem.at[slot, k])
+            for k, name in enumerate((*KEEP, *LEFT))
         ]
 
     def right_copies(slot, index):
@@ -538,8 +541,11 @@
             for k, name in enumerate(RIGHT)
         ]
 
-    def keep_load(slot, index):
-        return pltpu.make_async_copy(O.keep.at[index], R.keep.at[slot], R.k_sem.at[slot])
+    def keep_loads(slot, index):
+        return [
+            pltpu.make_async_copy(O[name].at[index], R[name].at[slot], R.k_sem.at[slot, k])
+            for k, name in enumerate(KEEP)
+        ]
 
     def turn_out():
         value = R.h[...]
@@ -566,6 +572,11 @@
                 for d in range(1, chips):
                     far_forward(d, item).start()
 
+            @pl.when(k > 0)
+            def _():
+                for copy in left_copies(1, 2 * item - 1):
+                    copy.start()
+
             R.h[...] = R.fin[item].astype(F32)
 
             def one(f, carry):
@@ -574,25 +585,24 @@
                     for copy in left_copies(f, 2 * (item - 1) + f):
                         copy.wait()
 
-                fresh = jnp.logical_not(early) & (item == 0) & (f == 0)
+                fresh = is_first & (item == 0) & (f == 0)
 
                 def arrived(name):
-                    if name not in early_names:
-
-                        @pl.when(fresh & is_first)
-                        def _():
-                            weight_copies[DOWN].wait()
-                            flip(W.dnT, W.dn)
-
+                    if name in early_names[:-1]:
+                        weight_copies[name].wait()
+                    elif name in early_names:
+                        pl.when(jnp.logical_not(held))(weight_copies[name].wait)
                     else:
-
-                        waits = fresh & jnp.logical_not(held) if name == early_names[-1] else fresh
-
-                        @pl.when(waits)
-                        def _():
-                            weight_copies[name].wait()
-
-                block_forward(W, views(f), arrived)
+                        weight_copies[DOWN].wait()
+                        flip(W.dnT, W.dn)
+
+                @pl.when(fresh)
+                def _():
+                    block_forward(W, views(f), arrived)
+
+                @pl.when(jnp.logical_not(fresh))
+                def _():
+                    block_forward(W, views(f), lambda name: None)
 
                 @pl.when(f == 0)
                 def _():
@@ -619,17 +629,18 @@
                 turn_out()
                 out_copy(item).start()
 
-            for copy in left_copies(1, 2 * item + 1):
-                copy.start()
             return carry
 
         lax.fori_loop(0, count, step, 0)
+        for copy in left_copies(1, 2 * (start + count) - 1):
+            copy.start()
         for f in range(2):
             for copy in left_copies(f, 2 * (start + count - 1) + f):
                 copy.wait()
 
     def backward_phase(start, count, is_far):
-        keep_load(1, 2 * start + 1).start()
+        for copy in keep_loads(1, 2 * start + 1):
+            copy.start()
 
         def step(k, carry):
             item = start + k
@@ -649,19 +660,27 @@
                 for d in range(1, chips):
                     far_backward(d, item).start()
 
+            @pl.when(k > 0)
+            def _():
+                for copy in right_copies(0, 2 * item - 2):
+                    copy.start()
+
             R.h[...] = R.bin[item].astype(F32) * R.valid[:, 0:1]
 
             def one(i, carry):
                 f = 1 - i
-                keep_load(f, 2 * item + f).wait()
+                for copy in keep_loads(f, 2 * item + f):
+                    copy.wait()
 
                 @pl.when(f == 1)
                 def _():
-                    keep_load(0, 2 * item).start()
+                    for copy in keep_loads(0, 2 * item):
+                        copy.start()
 
                 @pl.when((f == 0) & (k < count - 1))
                 def _():
-                    keep_load(1, 2 * item + 3).start()
+                    for copy in keep_loads(1, 2 * item + 3):
+                        copy.start()
 
                 @pl.when(k > 0)
                 def _():
@@ -702,11 +721,11 @@
                 turn_out()
                 grad_copy(item).start()
 
-            for copy in right_copies(0, 2 * item):
-                copy.start()
             return carry
 
         lax.fori_loop(0, count, step, 0)
+        for copy in right_copies(0, 2 * (start + count - 1)):
+            copy.start()
         for f in range(2):
             for copy in right_copies(f, 2 * (start + count - 1) + f):
                 copy.wait()
@@ -726,9 +745,6 @@
         def _():
             weight_copies[DOWN].wait()
             flip(W.dnT, W.dn)
-
-        @pl.when((p == 0) & early)
-        def _():
             for name in early_names:
                 weight_copies[name].wait()
 
@@ -815,7 +831,7 @@
         outs=vmem(own, ROWS, D),
         flip=vmem(D, ROWS),
         meta=vmem(items, 8, TILE, dtype=F32),
-        keep=vmem(2, ROWS, KEEP_WIDTH),
+        mine=vmem(own, 8, TILE, dtype=F32),
         h=vmem(ROWS, D, dtype=F32),
         e=vmem(ROWS, 1024, dtype=F32),
         gm=vmem(ROWS, 1024),
@@ -825,7 +841,7 @@
         bias=vmem(ROWS, TILE, dtype=F32),
         valid=vmem(ROWS, TILE, dtype=F32),
     )
-    for name, width in {**LEFT, **RIGHT}.items():
+    for name, width in {**KEEP, **LEFT, **RIGHT}.items():
         scratch[name] = vmem(2, ROWS, width)
     for name, (depth, width) in WEIGHTS.items():
         scratch["w_" + name] = vmem(depth, width)
@@ -845,17 +861,16 @@
         g_sem=(own,),
         oa_sem=(own,),
         ga_sem=(own,),
-        l_sem=(2, 1 + len(LEFT)),
+        l_sem=(2, len(KEEP) + len(LEFT)),
         r_sem=(2, len(RIGHT)),
-        k_sem=(2,),
+        k_sem=(2, len(KEEP)),
     )
     for name, shape in counts.items():
         scratch[name] = pltpu.SemaphoreType.DMA(shape)
     scratch.t_sem = pltpu.SemaphoreType.DMA
     shapes = Box(out=(D, own * ROWS), gin=(D, own * ROWS))
-    for name, width in {**LEFT, **RIGHT}.items():
+    for name, width in {**KEEP, **LEFT, **RIGHT}.items():
         shapes[name] = (2 * items, ROWS, width)
-    shapes.keep = (2 * items, ROWS, KEEP_WIDTH)
     out_shape = Box({name: jax.ShapeDtypeStruct(shape, BF) for name, shape in shapes.items()})
     out_shape.gga = out_shape.ggf = jax.ShapeDtypeStruct((1, D), F32)
     names = [[*hbm_inputs, *inputs], list(out_shape), list(scratch)]
@@ -1100,13 +1115,10 @@
     groups = lax.axis_size("dp")
     chips = groups // 2
     own = tokens.shape[0] // ROWS
-    meta = seq_counts.astype(F32).reshape(own, MICROS, 2).transpose(0, 2, 1)
-    meta = jnp.pad(meta.reshape(own, 2 * MICROS), ((0, 0), (0, 8 - 2 * MICROS)))
-    meta = jnp.broadcast_to(meta[:, :, None], (own, 8, TILE))
     cosl, sinl, coss, sins = rotary_tables()
     hbm_inputs = Box(tok=tokens.T, cot=cotangent.T, dnT=w_down[0].T)
     hbm_inputs.update(qkv=w_qkv[0], out=w_out[0], gu=w_gate_up[0])
-    inputs = Box(meta=meta, ga=attn_gain, gf=ffn_gain)
+    inputs = Box(counts=seq_counts.T, ga=attn_gain, gf=ffn_gain)
     inputs.update(cosl=cosl, sinl=sinl, coss=coss, sins=sins)
     O = run_pipeline(sections, chips, own, hbm_inputs, inputs)
     share = D // groups

time: 311 us -> 308 us (level)
  no operation moved by 1% of the time
where the time goes in v4:
time: 308 us; the launch traced here: 306 us
  Pallas kernels  305 us (99%)
    pallas_call x1, Pallas kernels, run_pipeline(): pl.pallas_call(functools.partial(pipeline_kernel, sections, chips, own, n...  273 us
    pallas_call x1, Pallas kernels, run_gradients(): pl.pallas_call(functools.partial(gradient_kernel, depth, share, names), o...  25.7 us
    pallas_call x1, Pallas kernels, run_finish(): pl.pallas_call(functools.partial(finish_kernel, groups, share, names), ou...  6.84 us

profile of v4, /device:TPU:0, one launch (start us, length us, event | category | flops | bytes accessed | tf_op | source)
XLA Modules:
  0.0 306.3 jit_solution(12437170720635753901)
XLA Ops:
  0.6 272.9 %shard_map.188 = (bf16[960,256]{1,0:T(8,128)(2,1)}, bf16[960,256]{1,0:T(8,128)(2,1)}, bf16[8,128,960]{2,1,0:T(8,128)(2,1)}, bf16[8,128,960]{2,1,0:T(8,128)(2,1)}...) custom-call(bf16[960,256]{1,0:T(8,128)(2,1)} %bitcast.41, ...), custom_call_target="tpu_custom_call" | custom-call | tf_op jit(solution)/shard_map/pallas_call | solution.py:877
  273.6 25.7 %shard_map.189 = (bf16[240,960]{1,0:T(8,128)(2,1)}, bf16[240,1600]{1,0:T(8,128)(2,1)}, bf16[240,2560]{1,0:T(8,128)(2,1)}, bf16[240,5120]{1,0:T(8,128)(2,1)}, f32[2,960]{1,0:T(2,128)}) custom-call(bf16[1024,960]{1,0:T(8,128)(2,1)} %bitcast.38, bf16[1024,960]{1,0:T(8,128)(2,1)} %bitcast.36, bf16[1024,960]{1,0:T(8,128)(2,1)} %bitcast.35, ...), custom_call_target="tpu_custom_call" | custom-call | tf_op jit(solution)/shard_map/pallas_call | solution.py:995
  299.3 6.8 %shard_map.190 = (f32[960,240]{1,0:T(8,128)}, f32[240,1600]{1,0:T(8,128)}, f32[240,2560]{1,0:T(8,128)}, f32[240,5120]{1,0:T(8,128)}, bf16[960,256]{1,0:T(8,128)(...) custom-call(bf16[240,960]{1,0:T(8,128)(2,1)} %get-tuple-element.43.refs_0_, ...), custom_call_target="tpu_custom_call" | custom-call | tf_op jit(solution)/shard_map/pallas_call | solution.py:1082

commit v5 on v4

--- a/solution.py
+++ b/solution.py
@@ -38,7 +38,7 @@
 V_HALF = 20
 MESH = pl.DeviceIdType.MESH
 DOWN = "dnT"
-HELD = 12
+HELD = 9
 
 KEEP = dict(x=D, mid=D, p=1024, qkv=1664, A=FF, B=FF)
 LEFT = dict(n1=D, mix=D, n2=D, hid=FF)
@@ -907,12 +907,14 @@
     loads = {
         name: pltpu.make_async_copy(I[name], R[name], R.load.at[k]) for k, name in enumerate(order)
     }
-    for name in order[:4]:
+    for name in order[:2]:
         loads[name].start()
     later = order[4:]
     R.gain[0:1] = I.gga[...]
     R.gain[1:2] = I.ggf[...]
     pl.semaphore_wait(barrier, 1)
+    for name in order[2:4]:
+        loads[name].start()
 
     def to_sibling(source, target, send, recv):
         return pltpu.make_async_remote_copy(
@@ -933,40 +935,63 @@
 
     mine = pl.ds(pl.multiple_of((2 * chip + core) * share, 16), share)
     other = pl.ds(pl.multiple_of((2 * chip + 1 - core) * share, 16), share)
-    base = 0
-    bases = {}
-    for name, (left, right, width) in PRODUCTS.items():
-        turned = R["t_" + left]
-        loads[left].wait()
+    def turn_left(left):
         for r, rw in chunks(depth):
             for c, w in chunks(D):
-                turned[c : c + w, r : r + rw] = R[left][r : r + rw, c : c + w].T
+                R["t_" + left][c : c + w, r : r + rw] = R[left][r : r + rw, c : c + w].T
+
+    bases, writes = {}, []
+    products = list(PRODUCTS.items())
+    lefts = [left for left, _, _ in PRODUCTS.values()]
+
+    def span_columns(name, first, n, width):
+        c = (first - bases[name]) * CHUNK
+        return slice(c, min(c + n * CHUNK, width))
+
+    def give(name, left, right, width):
+        for first, n in spans_of(bases[name], width):
+            columns = span_columns(name, first, n, width)
+            for i, (c, w) in enumerate(chunks(columns.stop - columns.start)):
+                c += columns.start
+                value = nn(R["t_" + left][other, :], R[right][:, c : c + w])
+                R.sent[first + i, :, 0:w] = value.astype(BF)
+            span_copy(first, n).start()
+
+    def take(name, left, right, width):
+        for first, n in spans_of(bases[name], width):
+            span_copy(first, n).wait_recv()
+            columns = span_columns(name, first, n, width)
+            for i, (c, w) in enumerate(chunks(columns.stop - columns.start)):
+                c += columns.start
+                total = nn(R["t_" + left][mine, :], R[right][:, c : c + w])
+                total = total + R.got[first + i, :, 0:w].astype(F32)
+                R["sum_" + name][:, c : c + w] = total.astype(BF)
+            place = R["sum_" + name].at[:, columns], O[name].at[:, columns]
+            writes.append(pltpu.make_async_copy(*place, R.write.at[len(writes)]))
+            writes[-1].start()
+
+    base = 0
+    for k, (name, (left, right, width)) in enumerate(products):
+        bases[name] = base
+        base += len(chunks(width))
+        loads[left].wait()
+        turn_left(left)
         loads[right].wait()
         for more in later[:2]:
             loads[more].start()
         later = later[2:]
-        for first, n in spans_of(base, width):
-            for i in range(first, first + n):
-                c = (i - base) * CHUNK
-                w = min(CHUNK, width - c)
-                R.sent[i, :, 0:w] = nn(turned[other, :], R[right][:, c : c + w]).astype(BF)
-            span_copy(first, n).start()
-        bases[name] = base
-        base += len(chunks(width))
-    for name, (left, right, width) in PRODUCTS.items():
-        base = bases[name]
-        for first, n in spans_of(base, width):
-            span_copy(first, n).wait_recv()
-            for i in range(first, first + n):
-                c = (i - base) * CHUNK
-                w = min(CHUNK, width - c)
-                total = nn(R["t_" + left][mine, :], R[right][:, c : c + w])
-                O[name][:, c : c + w] = (total + R.got[i, :, 0:w].astype(F32)).astype(BF)
+        give(name, left, right, width)
+        if k > 0:
+            before, spec = products[k - 1]
+            take(before, *spec)
+    take(products[-1][0], *products[-1][1])
     gain_copy.wait()
     O.gain[...] = R.gain[...] + R.got_gain[...]
     for name, (_, _, width) in PRODUCTS.items():
         for first, n in spans_of(bases[name], width):
             span_copy(first, n).wait_send()
+    for write in writes:
+        write.wait()
 
 
 def run_gradients(share, operands, gga, ggf):
@@ -974,14 +999,16 @@
     order = [n for pair in PRODUCTS.values() for n in pair[:2]]
     blocks = sum(len(chunks(width)) for _, _, width in PRODUCTS.values())
     scratch = Box({n: vmem(*operands[n].shape) for n in order})
-    for left, _, _ in PRODUCTS.values():
+    for name, (left, _, width) in PRODUCTS.items():
         scratch["t_" + left] = vmem(D, depth)
+        scratch["sum_" + name] = vmem(share, width)
     scratch.update(
         sent=vmem(blocks, share, CHUNK),
         got=vmem(blocks, share, CHUNK),
         gain=vmem(2, D, dtype=F32),
         got_gain=vmem(2, D, dtype=F32),
         load=pltpu.SemaphoreType.DMA((len(order),)),
+        write=pltpu.SemaphoreType.DMA((blocks,)),
         ss=pltpu.SemaphoreType.DMA((blocks,)),
         rs=pltpu.SemaphoreType.DMA((blocks,)),
         gs=pltpu.SemaphoreType.DMA,
@@ -996,7 +1023,7 @@
         functools.partial(gradient_kernel, depth, share, names),
         out_shape=list(shapes.values()),
         in_specs=[HBM] * len(order) + [LOCAL] * 2,
-        out_specs=[LOCAL] * len(shapes),
+        out_specs=[HBM] * len(PRODUCTS) + [LOCAL],
         scratch_shapes=list(scratch.values()),
         compiler_params=pltpu.CompilerParams(
             collective_id=1, has_side_effects=True, vmem_limit_bytes=VMEM_LIMIT

time: 308 us -> 306 us (level)
  no operation moved by 1% of the time
where the time goes in v5:
time: 306 us
  Pallas kernels  305 us (100%)
    pallas_call x1, Pallas kernels, run_pipeline(): pl.pallas_call(functools.partial(pipeline_kernel, sections, chips, own, n...  273 us
    pallas_call x1, Pallas kernels, run_gradients(): pl.pallas_call(functools.partial(gradient_kernel, depth, share, names), o...  25.1 us
    pallas_call x1, Pallas kernels, run_finish(): pl.pallas_call(functools.partial(finish_kernel, groups, share, names), ou...  6.84 us

profile of v5, /device:TPU:0, one launch (start us, length us, event | category | flops | bytes accessed | tf_op | source)
XLA Modules:
  0.0 305.7 jit_solution(16524766935379879323)
XLA Ops:
  0.6 272.9 %shard_map.188 = (bf16[960,256]{1,0:T(8,128)(2,1)}, bf16[960,256]{1,0:T(8,128)(2,1)}, bf16[8,128,960]{2,1,0:T(8,128)(2,1)}, bf16[8,128,960]{2,1,0:T(8,128)(2,1)}...) custom-call(bf16[960,256]{1,0:T(8,128)(2,1)} %bitcast.41, ...), custom_call_target="tpu_custom_call" | custom-call | tf_op jit(solution)/shard_map/pallas_call | solution.py:877
  273.6 25.1 %shard_map.189 = (bf16[240,960]{1,0:T(8,128)(2,1)}, bf16[240,1600]{1,0:T(8,128)(2,1)}, bf16[240,2560]{1,0:T(8,128)(2,1)}, bf16[240,5120]{1,0:T(8,128)(2,1)}, f32[2,960]{1,0:T(2,128)}) custom-call(bf16[1024,960]{1,0:T(8,128)(2,1)} %bitcast.38, bf16[1024,960]{1,0:T(8,128)(2,1)} %bitcast.36, bf16[1024,960]{1,0:T(8,128)(2,1)} %bitcast.35, ...), custom_call_target="tpu_custom_call" | custom-call | tf_op jit(solution)/shard_map/pallas_call | solution.py:1022
  298.7 6.8 %shard_map.190 = (f32[960,240]{1,0:T(8,128)}, f32[240,1600]{1,0:T(8,128)}, f32[240,2560]{1,0:T(8,128)}, f32[240,5120]{1,0:T(8,128)}, bf16[960,256]{1,0:T(8,128)(...) custom-call(bf16[240,960]{1,0:T(8,128)(2,1)} %get-tuple-element.43.refs_0_, ...), custom_call_target="tpu_custom_call" | custom-call | tf_op jit(solution)/shard_map/pallas_call | solution.py:1109

commit v6 on v5

--- a/solution.py
+++ b/solution.py
@@ -585,7 +585,7 @@
                     for copy in left_copies(f, 2 * (item - 1) + f):
                         copy.wait()
 
-                fresh = is_first & (item == 0) & (f == 0)
+                fresh = is_first & (item == 0)
 
                 def arrived(name):
                     if name in early_names[:-1]:
@@ -596,13 +596,18 @@
                         weight_copies[DOWN].wait()
                         flip(W.dnT, W.dn)
 
-                @pl.when(fresh)
-                def _():
-                    block_forward(W, views(f), arrived)
-
-                @pl.when(jnp.logical_not(fresh))
-                def _():
+                def forward():
                     block_forward(W, views(f), lambda name: None)
+
+                if f == 0:
+
+                    @pl.when(fresh)
+                    def _():
+                        block_forward(W, views(f), arrived)
+
+                    pl.when(jnp.logical_not(fresh))(forward)
+                else:
+                    forward()
 
                 @pl.when(f == 0)
                 def _():
@@ -611,7 +616,8 @@
 
                 return carry
 
-            lax.fori_loop(0, 2, one, 0)
+            for f in range(2):
+                one(f, 0)
 
             @pl.when(jnp.logical_not(is_far))
             def _():
@@ -696,7 +702,8 @@
 
                 return carry
 
-            lax.fori_loop(0, 2, one, 0)
+            for i in range(2):
+                one(i, 0)
 
             @pl.when(jnp.logical_not(is_far))
             def _():

time: 306 us -> 301 us (0.984)
  Pallas kernels: 305 us -> 300 us
    pallas_call x1, Pallas kernels: 273 us -> 268 us  [run_pipeline(): pl.pallas_call(functools.partial(pipeline_kernel, sections, chips, own, n...]
where the time goes in v6:
time: 301 us
  Pallas kernels  300 us (100%)
    pallas_call x1, Pallas kernels, run_pipeline(): pl.pallas_call(functools.partial(pipeline_kernel, sections, chips, own, n...  268 us
    pallas_call x1, Pallas kernels, run_gradients(): pl.pallas_call(functools.partial(gradient_kernel, depth, share, names), o...  25.1 us
    pallas_call x1, Pallas kernels, run_finish(): pl.pallas_call(functools.partial(finish_kernel, groups, share, names), ou...  6.84 us

profile of v6, /device:TPU:0, one launch (start us, length us, event | category | flops | bytes accessed | tf_op | source)
XLA Modules:
  0.0 301.1 jit_solution(16442444558239689312)
XLA Ops:
  0.6 268.4 %shard_map.188 = (bf16[960,256]{1,0:T(8,128)(2,1)}, bf16[960,256]{1,0:T(8,128)(2,1)}, bf16[8,128,960]{2,1,0:T(8,128)(2,1)}, bf16[8,128,960]{2,1,0:T(8,128)(2,1)}...) custom-call(bf16[960,256]{1,0:T(8,128)(2,1)} %bitcast.41, ...), custom_call_target="tpu_custom_call" | custom-call | tf_op jit(solution)/shard_map/pallas_call | solution.py:884
  269.0 25.1 %shard_map.189 = (bf16[240,960]{1,0:T(8,128)(2,1)}, bf16[240,1600]{1,0:T(8,128)(2,1)}, bf16[240,2560]{1,0:T(8,128)(2,1)}, bf16[240,5120]{1,0:T(8,128)(2,1)}, f32[2,960]{1,0:T(2,128)}) custom-call(bf16[1024,960]{1,0:T(8,128)(2,1)} %bitcast.38, bf16[1024,960]{1,0:T(8,128)(2,1)} %bitcast.36, bf16[1024,960]{1,0:T(8,128)(2,1)} %bitcast.35, ...), custom_call_target="tpu_custom_call" | custom-call | tf_op jit(solution)/shard_map/pallas_call | solution.py:1029
  294.1 6.8 %shard_map.190 = (f32[960,240]{1,0:T(8,128)}, f32[240,1600]{1,0:T(8,128)}, f32[240,2560]{1,0:T(8,128)}, f32[240,5120]{1,0:T(8,128)}, bf16[960,256]{1,0:T(8,128)(...) custom-call(bf16[240,960]{1,0:T(8,128)(2,1)} %get-tuple-element.43.refs_0_, ...), custom_call_target="tpu_custom_call" | custom-call | tf_op jit(solution)/shard_map/pallas_call | solution.py:1116
